TPU v7x, 512 devices: a whole 4x4x16 slice. The times are simulated.
512 devices in a mesh: pipe: 8 (over x, core), blk: 32 (over z, y_hi), uly: 2 (over y_lo).
Axes of the slice: x: 4, y: 4 (y_hi: 2, y_lo: 2; y = y_hi * 2 + y_lo), z: 16, core: 2. Of those that a mesh axis runs over, the one named last changes fastest.
Arguments:
- slot_order: int32 [64], replicated, may hold values from 0 to 63, each once
- query_fwd: bfloat16 [8, 4096, 4096], P('pipe', ('blk', 'uly')), may hold values from -5 to 5
- key_fwd: bfloat16 [8, 4096, 512], P('pipe', ('blk', 'uly')), may hold values from -5 to 5
- value_forward: bfloat16 [8, 4096, 512], P('pipe', ('blk', 'uly')), may hold values from -6 to 6
- query_bwd: bfloat16 [8, 4096, 4096], P('pipe', ('blk', 'uly')), may hold values from -5 to 5
- key_bwd: bfloat16 [8, 4096, 512], P('pipe', ('blk', 'uly')), may hold values from -5 to 5
- value_backward: bfloat16 [8, 4096, 512], P('pipe', ('blk', 'uly')), may hold values from -6 to 6
- out_grad: bfloat16 [8, 4096, 4096], P('pipe', ('blk', 'uly')), may hold values from -6 to 6
Outputs:
- handed: bfloat16 [8, 4096, 4096], P('pipe', ('blk', 'uly'))
- query_grad: bfloat16 [8, 4096, 4096], P('pipe', ('blk', 'uly'))
- key_grad: bfloat16 [8, 4096, 512], P('pipe', ('blk', 'uly'))
- value_grad: bfloat16 [8, 4096, 512], P('pipe', ('blk', 'uly'))
Inputs may be any that keep to these rules, and one draw needn't show every extreme that they name: `slot_order`: each slot holds a different part.
All inputs are finite; a program needn't handle non-finite values.
Results may differ from a plain program's by a relative error of at most 0.011.
Values may be sent and summed in bfloat16 or wider, within the bound.
A program may use at most 128 MiB of HBM per device.

v0:
```python
import jax
import jax.numpy as jnp
from jax import lax
from jax.sharding import PartitionSpec as P

HEAD_SIZE = 128
VISIBLE_GROUPS = 4
QUERY_PER_KEY = 8


NEG = -1e30


def shifted(value, axis, steps):
    count = lax.axis_size(axis)
    pairs = [(source, (source + steps) % count) for source in range(count)]
    return lax.ppermute(value, axis, pairs)


def from_behind(array, axis, by):
    peers = lax.axis_size(axis)
    pairs = [(i, i + by) for i in range(peers) if 0 <= i + by < peers]
    return lax.ppermute(array, axis, pairs)


def pass_keys(kv_block, distance):
    return shifted(kv_block, "blk", distance)


def send_grads(key_part, value_part, distance):
    return (
        shifted(key_part.astype(jnp.bfloat16), "blk", -distance).astype(key_part.dtype),
        shifted(value_part.astype(jnp.bfloat16), "blk", -distance).astype(value_part.dtype),
    )


def group_positions(slot_order, group_id, uly_size, tok_rows):
    row_index = jnp.arange(uly_size * tok_rows, dtype=jnp.int32)
    slot_ids = group_id * uly_size + row_index // tok_rows
    slot_range = jnp.arange(slot_order.shape[0], dtype=jnp.int32)
    placed = jnp.sum(
        jnp.where(slot_ids[:, None] == slot_range[None, :], slot_order[None, :], 0), axis=1
    )
    return placed * tok_rows + row_index % tok_rows


def head_scores(query_rows, key_row_block, allowed):
    raw_scores = jnp.einsum(
        "qgrd,kgd->grqk", query_rows, key_row_block, preferred_element_type=jnp.float32
    )
    return jnp.where(allowed[None, None], raw_scores * query_rows.shape[-1] ** (-0.5), NEG)


def flash_update(query_rows, kv_block, allowed, state):
    row_peak, row_total, running = state
    scores = head_scores(query_rows, kv_block[:, 0], allowed)
    new_peak = jnp.maximum(row_peak, jnp.max(scores, axis=-1))
    raised = jnp.exp(scores - new_peak[..., None])
    factor = jnp.exp(row_peak - new_peak)
    new_total = row_total * factor + jnp.sum(raised, axis=-1)
    block_out = jnp.einsum(
        "grqk,kgd->qgrd",
        raised.astype(jnp.bfloat16),
        kv_block[:, 1],
        preferred_element_type=jnp.float32,
    )
    return (new_peak, new_total, running * jnp.transpose(factor, (2, 0, 1))[..., None] + block_out)


def flash_pass(query_rows, kv_blocks, masks):
    stat_shape = (query_rows.shape[1], query_rows.shape[2], query_rows.shape[0])
    state = (
        jnp.full(stat_shape, NEG, jnp.float32),
        jnp.zeros(stat_shape, jnp.float32),
        jnp.zeros(query_rows.shape, jnp.float32),
    )
    for kv_block, allowed in zip(kv_blocks, masks):
        state = flash_update(query_rows, kv_block, allowed, state)
    return state


def block_grads(query_rows, upstream, kv_block, allowed, log_total, row_delta):
    key_row_block = kv_block[:, 0]
    scores = head_scores(query_rows, key_row_block, allowed)
    attn_probs = jnp.exp(scores - log_total[..., None])
    grad_probs = jnp.einsum(
        "qgrd,kgd->grqk", upstream, kv_block[:, 1], preferred_element_type=jnp.float32
    )
    grad_scores = (attn_probs * (grad_probs - row_delta[..., None])).astype(jnp.bfloat16)
    inv_root = query_rows.shape[-1] ** (-0.5)
    grad_query = (
        jnp.einsum("grqk,kgd->qgrd", grad_scores, key_row_block, preferred_element_type=jnp.float32)
        * inv_root
    )
    key_gradient = (
        jnp.einsum("grqk,qgrd->kgd", grad_scores, query_rows, preferred_element_type=jnp.float32)
        * inv_root
    )
    value_gradient = jnp.einsum(
        "grqk,qgrd->kgd",
        attn_probs.astype(jnp.bfloat16),
        upstream,
        preferred_element_type=jnp.float32,
    )
    return (grad_query, key_gradient, value_gradient)


def both_passes(
    query_first,
    query_second,
    upstream,
    blocks_fwd,
    blocks_bwd,
    masks,
    head_dims,
    key_shape,
    returner,
):
    row_peak, row_total, running = flash_pass(query_first, blocks_fwd, masks)
    attention = (running / jnp.transpose(row_total, (2, 0, 1))[..., None]).astype(jnp.bfloat16)
    peak_bwd, total_bwd, running_bwd = flash_pass(query_second, blocks_bwd, masks)
    weighted = running_bwd / jnp.transpose(total_bwd, (2, 0, 1))[..., None]
    log_total = peak_bwd + jnp.log(total_bwd)
    row_delta = jnp.transpose(jnp.sum(upstream.astype(jnp.float32) * weighted, axis=-1), (1, 2, 0))
    query_grad = jnp.zeros(head_dims, jnp.float32)
    key_sum = jnp.zeros(key_shape, jnp.float32)
    value_sum = jnp.zeros(key_shape, jnp.float32)
    for block_index in range(len(masks)):
        grad_query, key_gradient, value_gradient = block_grads(
            query_second,
            upstream,
            blocks_bwd[block_index],
            masks[block_index],
            log_total,
            row_delta,
        )
        query_grad = query_grad + grad_query
        returned = returner(block_index, key_gradient, value_gradient)
        key_sum = key_sum + returned[0]
        value_sum = value_sum + returned[1]
    return (attention, query_grad, key_sum, value_sum)


def group_plan(
    slot_order, query_fwd, key_fwd, value_forward, query_bwd, key_bwd, value_backward, out_grad
):
    uly_size = lax.axis_size("uly")
    group_count = lax.axis_size("blk")
    my_group = lax.axis_index("blk")
    tok_rows = query_fwd.shape[1]
    arrived = (
        lax.all_to_all(query_fwd[0], "uly", split_axis=1, concat_axis=0, tiled=True),
        lax.all_to_all(key_fwd[0], "uly", split_axis=1, concat_axis=0, tiled=True),
        lax.all_to_all(value_forward[0], "uly", split_axis=1, concat_axis=0, tiled=True),
        lax.all_to_all(query_bwd[0], "uly", split_axis=1, concat_axis=0, tiled=True),
        lax.all_to_all(key_bwd[0], "uly", split_axis=1, concat_axis=0, tiled=True),
        lax.all_to_all(value_backward[0], "uly", split_axis=1, concat_axis=0, tiled=True),
        lax.all_to_all(out_grad[0], "uly", split_axis=1, concat_axis=0, tiled=True),
    )
    span_rows = arrived[1].shape[0]
    kv_local = arrived[1].shape[1] // HEAD_SIZE
    head_dims = (span_rows, kv_local, QUERY_PER_KEY, HEAD_SIZE)
    key_shape = (span_rows, kv_local, HEAD_SIZE)
    query_first = arrived[0].reshape(head_dims)
    pair_fwd = jnp.stack([arrived[1].reshape(key_shape), arrived[2].reshape(key_shape)], axis=1)
    query_second = arrived[3].reshape(head_dims)
    pair_bwd = jnp.stack([arrived[4].reshape(key_shape), arrived[5].reshape(key_shape)], axis=1)
    upstream = arrived[6].reshape(head_dims)
    query_pos = group_positions(slot_order, my_group, uly_size, tok_rows)
    masks = []
    for cycle_step in range(VISIBLE_GROUPS):
        source_group = (my_group - cycle_step + group_count) % group_count
        masks.append(
            query_pos[:, None]
            >= group_positions(slot_order, source_group, uly_size, tok_rows)[None, :]
        )
    blocks_fwd, blocks_bwd = ([pair_fwd], [pair_bwd])
    for cycle_step in range(1, VISIBLE_GROUPS):
        distance, source_fwd, source_bwd = (1, blocks_fwd[-1], blocks_bwd[-1])
        blocks_fwd.append(pass_keys(source_fwd, distance))
        blocks_bwd.append(pass_keys(source_bwd, distance))

    def returner(block_index, key_gradient, value_gradient):
        if block_index == 0:
            return (key_gradient, value_gradient)
        return send_grads(key_gradient, value_gradient, block_index)

    attention, query_grad, key_sum, value_sum = both_passes(
        query_first,
        query_second,
        upstream,
        blocks_fwd,
        blocks_bwd,
        masks,
        head_dims,
        key_shape,
        returner,
    )
    return (
        lax.all_to_all(
            attention.reshape(span_rows, -1), "uly", split_axis=0, concat_axis=1, tiled=True
        ),
        lax.all_to_all(
            query_grad.astype(jnp.bfloat16).reshape(span_rows, -1),
            "uly",
            split_axis=0,
            concat_axis=1,
            tiled=True,
        ),
        lax.all_to_all(
            key_sum.astype(jnp.bfloat16).reshape(span_rows, -1),
            "uly",
            split_axis=0,
            concat_axis=1,
            tiled=True,
        ),
        lax.all_to_all(
            value_sum.astype(jnp.bfloat16).reshape(span_rows, -1),
            "uly",
            split_axis=0,
            concat_axis=1,
            tiled=True,
        ),
    )


def local(
    slot_order, query_fwd, key_fwd, value_forward, query_bwd, key_bwd, value_backward, out_grad
):
    finished = group_plan(
        slot_order, query_fwd, key_fwd, value_forward, query_bwd, key_bwd, value_backward, out_grad
    )
    handed = from_behind(finished[0], "pipe", 1)
    return (handed[None], finished[1][None], finished[2][None], finished[3][None])


def solution(mesh):
    return jax.shard_map(
        local,
        mesh=mesh,
        in_specs=(
            P(),
            P("pipe", ("blk", "uly"), None),
            P("pipe", ("blk", "uly"), None),
            P("pipe", ("blk", "uly"), None),
            P("pipe", ("blk", "uly"), None),
            P("pipe", ("blk", "uly"), None),
            P("pipe", ("blk", "uly"), None),
            P("pipe", ("blk", "uly"), None),
        ),
        out_specs=(
            P("pipe", ("blk", "uly"), None),
            P("pipe", ("blk", "uly"), None),
            P("pipe", ("blk", "uly"), None),
            P("pipe", ("blk", "uly"), None),
        ),
        check_vma=False,
    )
```

profile of v0, /device:TPU:2, one launch (start us, length us, event | category | flops | bytes accessed | tf_op | source)
XLA Modules:
  0.0 178.3 jit_solution(15949830455302627981)
XLA Ops:
  2.1 3.3 %all-to-all-start.4 = ((bf16[64,2,256]{2,0,1:T(8,128)(2,1)}), bf16[64,2,256]{2,0,1:T(8,128)(2,1)S(1)}, u32[]{:S(2)}, u32[]{:S(2)}) async-start(bf16[64,2,256]{2,0,1:T(8,128)(2,1)} %copy.209), calls=%async_computation.4 | async-start | bytes 131072 | tf_op jit(solution)/shard_map/all_to_all | solution.py:156
  7.0 2.6 %all-to-all-done.4 = bf16[64,2,256]{2,0,1:T(8,128)(2,1)S(1)} async-done(((bf16[64,2,256]{2,0,1:T(8,128)(2,1)}), bf16[64,2,256]{2,0,1:T(8,128)(2,1)S(1)}, u32[]{:S(2)}, u32[]{:S(2)}) %all-to-all-start.4) | async-done | bytes 65568 | tf_op jit(solution)/shard_map/all_to_all | solution.py:156
  9.5 3.3 %all-to-all-start.6 = ((bf16[64,2,256]{2,0,1:T(8,128)(2,1)}), bf16[64,2,256]{2,0,1:T(8,128)(2,1)S(1)}, u32[]{:S(2)}, u32[]{:S(2)}) async-start(bf16[64,2,256]{2,0,1:T(8,128)(2,1)} %copy.213), calls=%async_computation.6 | async-start | bytes 131072 | tf_op jit(solution)/shard_map/all_to_all | solution.py:157
  13.6 3.3 %all-to-all-done.6 = bf16[64,2,256]{2,0,1:T(8,128)(2,1)S(1)} async-done(((bf16[64,2,256]{2,0,1:T(8,128)(2,1)}), bf16[64,2,256]{2,0,1:T(8,128)(2,1)S(1)}, u32[]{:S(2)}, u32[]{:S(2)}) %all-to-all-start.6) | async-done | bytes 65568 | tf_op jit(solution)/shard_map/all_to_all | solution.py:157
  17.0 3.3 %all-to-all-start = ((bf16[64,2,256]{2,0,1:T(8,128)(2,1)}), bf16[64,2,256]{2,0,1:T(8,128)(2,1)S(1)}, u32[]{:S(2)}, u32[]{:S(2)}) async-start(bf16[64,2,256]{2,0,1:T(8,128)(2,1)} %copy.186), calls=%async_computation | async-start | bytes 131072 | tf_op jit(solution)/shard_map/all_to_all | solution.py:153
  21.0 3.4 %all-to-all-done = bf16[64,2,256]{2,0,1:T(8,128)(2,1)S(1)} async-done(((bf16[64,2,256]{2,0,1:T(8,128)(2,1)}), bf16[64,2,256]{2,0,1:T(8,128)(2,1)S(1)}, u32[]{:S(2)}, u32[]{:S(2)}) %all-to-all-start) | async-done | bytes 65568 | tf_op jit(solution)/shard_map/all_to_all | solution.py:153
  24.4 3.3 %all-to-all-start.2 = ((bf16[64,2,256]{2,0,1:T(8,128)(2,1)}), bf16[64,2,256]{2,0,1:T(8,128)(2,1)S(1)}, u32[]{:S(2)}, u32[]{:S(2)}) async-start(bf16[64,2,256]{2,0,1:T(8,128)(2,1)} %copy.190), calls=%async_computation.2 | async-start | bytes 131072 | tf_op jit(solution)/shard_map/all_to_all | solution.py:154
  31.9 3.5 %all-to-all-start.5 = ((bf16[64,2,2048]{2,0,1:T(8,128)(2,1)}), bf16[64,2,2048]{2,0,1:T(8,128)(2,1)S(1)}, u32[]{:S(2)}, u32[]{:S(2)}) async-start(bf16[64,2,2048]{2,0,1:T(8,128)(2,1)} %copy.210), calls=%async_computation.5 | async-start | bytes 1048576 | tf_op jit(solution)/shard_map/all_to_all | solution.py:155
  35.5 5.1 %collective-permute-start.4 = (bf16[128,2,2,128]{3,0,2,1:T(8,128)(2,1)S(1)}, bf16[128,2,2,128]{3,0,2,1:T(8,128)(2,1)S(1)}, u32[]{:S(2)}, u32[]{:S(2)}) collective-permute-start(bf16[128,2,2,128]{3,0,2,1:T(8,128)(2,1)S(1)} %pad_maximum_fusion.1), channel_id=1, source_target_pairs={{0,2},{2,4},{4,6},{6,8},{8,10},{10,12},{12,14},{14,16},{16,18},{18... | collective-permute-start | bytes 393224 | tf_op jit(solution)/shard_map/ppermute | solution.py:17
  40.7 2.2 %all-to-all-done.5 = bf16[64,2,2048]{2,0,1:T(8,128)(2,1)S(1)} async-done(((bf16[64,2,2048]{2,0,1:T(8,128)(2,1)}), bf16[64,2,2048]{2,0,1:T(8,128)(2,1)S(1)}, u32[]{:S(2)}, u32[]{:S(2)}) %all-to-all-start.5) | async-done | bytes 524320 | tf_op jit(solution)/shard_map/all_to_all | solution.py:155
  42.9 3.5 %all-to-all-start.1 = ((bf16[64,2,2048]{2,0,1:T(8,128)(2,1)}), bf16[64,2,2048]{2,0,1:T(8,128)(2,1)S(1)}, u32[]{:S(2)}, u32[]{:S(2)}) async-start(bf16[64,2,2048]{2,0,1:T(8,128)(2,1)} %copy.187), calls=%async_computation.1 | async-start | bytes 1048576 | tf_op jit(solution)/shard_map/all_to_all | solution.py:152
  46.4 4.2 %collective-permute-start = (bf16[128,2,2,128]{3,0,2,1:T(8,128)(2,1)S(1)}, bf16[128,2,2,128]{3,0,2,1:T(8,128)(2,1)}, u32[]{:S(2)}, u32[]{:S(2)}) collective-permute-start(bf16[128,2,2,128]{3,0,2,1:T(8,128)(2,1)S(1)} %pad_maximum_fusion), channel_id=1, source_target_pairs={{0,2},{2,4},{4,6},{6,8},{8,10},{10,12},{12,14},{14,16},{16,18},{18... | collective-permute-start | bytes 393224 | tf_op jit(solution)/shard_map/ppermute | solution.py:17
  52.6 4.1 %collective-permute-start.5 = (bf16[128,2,2,128]{3,0,2,1:T(8,128)(2,1)S(1)}, bf16[128,2,2,128]{3,0,2,1:T(8,128)(2,1)S(1)}, u32[]{:S(2)}, u32[]{:S(2)}) collective-permute-start(bf16[128,2,2,128]{3,0,2,1:T(8,128)(2,1)S(1)} %collective-permute-done.4), channel_id=1, source_target_pairs={{0,2},{2,4},{4,6},{6,8},{8,10},{10,12},{12,14},{14,16},{16,18},{18... | collective-permute-start | bytes 393224 | tf_op jit(solution)/shard_map/ppermute | solution.py:17
  56.7 6.0 %collective-permute-done = bf16[128,2,2,128]{3,0,2,1:T(8,128)(2,1)} collective-permute-done((bf16[128,2,2,128]{3,0,2,1:T(8,128)(2,1)S(1)}, bf16[128,2,2,128]{3,0,2,1:T(8,128)(2,1)}, u32[]{:S(2)}, u32[]{:S(2)}) %collective-permute-start) | collective-permute-done | bytes 131104 | tf_op jit(solution)/shard_map/ppermute | solution.py:17
  64.8 4.2 %all-to-all-start.7 = ((bf16[64,2,2048]{2,0,1:T(8,128)(2,1)}), bf16[64,2,2048]{2,0,1:T(8,128)(2,1)}, u32[]{:S(2)}, u32[]{:S(2)}) async-start(bf16[64,2,2048]{2,0,1:T(8,128)(2,1)} %copy.219), calls=%async_computation.7 | async-start | bytes 1048576 | tf_op jit(solution)/shard_map/all_to_all | solution.py:158
  71.7 2.8 %fusion.159 = (f32[2,8,128]{2,1,0:T(8,128)}, f32[2,8,128,128]{2,3,1,0:T(8,128)}) fusion(bf16[128,2,8,128]{3,2,1,0:T(8,128)(2,1)S(1)} %bitcast.523, bf16[128,2,2,128]{3,0,2,1:T(8,128)(2,1)} %collective-permute-done, pred[128,128]{0,1:T(8,128)(4,1)S(1)} %copy-done.18), kind=kOutput, calls=%fused_computation.252 | convolution fusion | flops 67893248 | bytes 1662976 | tf_op jit(solution)/shard_map/qgrd,kgd->grqk/dot_general | solution.py:48
  79.1 2.8 %collective-permute-start.6 = (bf16[128,2,2,128]{3,0,2,1:T(8,128)(2,1)S(1)}, bf16[128,2,2,128]{3,0,2,1:T(8,128)(2,1)S(1)}, u32[]{:S(2)}, u32[]{:S(2)}) collective-permute-start(bf16[128,2,2,128]{3,0,2,1:T(8,128)(2,1)S(1)} %collective-permute-done.5), channel_id=1, source_target_pairs={{0,2},{2,4},{4,6},{6,8},{8,10},{10,12},{12,14},{14,16},{16,18},{18... | collective-permute-start | bytes 393224 | tf_op jit(solution)/shard_map/ppermute | solution.py:17
  84.2 2.3 %collective-permute-start.2 = (bf16[128,2,2,128]{3,0,2,1:T(8,128)(2,1)}, bf16[128,2,2,128]{3,0,2,1:T(8,128)(2,1)S(1)}, u32[]{:S(2)}, u32[]{:S(2)}) collective-permute-start(bf16[128,2,2,128]{3,0,2,1:T(8,128)(2,1)} %collective-permute-done.1), channel_id=1, source_target_pairs={{0,2},{2,4},{4,6},{6,8},{8,10},{10,12},{12,14},{14,16},{16,18},{18... | collective-permute-start | bytes 393224 | tf_op jit(solution)/shard_map/ppermute | solution.py:17
  86.6 3.0 %collective-permute-done.6 = bf16[128,2,2,128]{3,0,2,1:T(8,128)(2,1)S(1)} collective-permute-done((bf16[128,2,2,128]{3,0,2,1:T(8,128)(2,1)S(1)}, bf16[128,2,2,128]{3,0,2,1:T(8,128)(2,1)S(1)}, u32[]{:S(2)}, u32[]{:S(2)}) %collective-permute-start.6) | collective-permute-done | bytes 131104 | tf_op jit(solution)/shard_map/ppermute | solution.py:17
  93.5 7.7 %collective-permute-start.12 = (bf16[128,2,128]{2,0,1:T(8,128)(2,1)}, bf16[128,2,128]{2,0,1:T(8,128)(2,1)}, u32[]{:S(2)}, u32[]{:S(2)}) collective-permute-start(bf16[128,2,128]{2,0,1:T(8,128)(2,1)} %fusion.66), channel_id=1, source_target_pairs={{0,58},{2,60},{4,62},{6,0},{8,2},{10,4},{12,6},{14,8},{16,10},{18,... | collective-permute-start | bytes 196616 | tf_op jit(solution)/shard_map/ppermute | solution.py:17
  101.2 4.6 %collective-permute-start.11 = (bf16[128,2,128]{2,0,1:T(8,128)(2,1)}, bf16[128,2,128]{2,0,1:T(8,128)(2,1)}, u32[]{:S(2)}, u32[]{:S(2)}) collective-permute-start(bf16[128,2,128]{2,0,1:T(8,128)(2,1)} %fusion.67), channel_id=1, source_target_pairs={{0,60},{2,62},{4,0},{6,2},{8,4},{10,6},{12,8},{14,10},{16,12},{18,... | collective-permute-start | bytes 196616 | tf_op jit(solution)/shard_map/ppermute | solution.py:17
  105.8 2.6 %collective-permute-start.10 = (bf16[128,2,128]{2,0,1:T(8,128)(2,1)}, bf16[128,2,128]{2,0,1:T(8,128)(2,1)}, u32[]{:S(2)}, u32[]{:S(2)}) collective-permute-start(bf16[128,2,128]{2,0,1:T(8,128)(2,1)} %fusion.68), channel_id=1, source_target_pairs={{0,62},{2,0},{4,2},{6,4},{8,6},{10,8},{12,10},{14,12},{16,14},{18,... | collective-permute-start | bytes 196616 | tf_op jit(solution)/shard_map/ppermute | solution.py:17
  111.5 6.7 %collective-permute-start.9 = (bf16[128,2,128]{2,0,1:T(8,128)(2,1)}, bf16[128,2,128]{2,0,1:T(8,128)(2,1)}, u32[]{:S(2)}, u32[]{:S(2)}) collective-permute-start(bf16[128,2,128]{2,0,1:T(8,128)(2,1)} %fusion.71), channel_id=1, source_target_pairs={{0,58},{2,60},{4,62},{6,0},{8,2},{10,4},{12,6},{14,8},{16,10},{18,... | collective-permute-start | bytes 196616 | tf_op jit(solution)/shard_map/ppermute | solution.py:17
  120.9 4.3 %collective-permute-start.8 = (bf16[128,2,128]{2,0,1:T(8,128)(2,1)}, bf16[128,2,128]{2,0,1:T(8,128)(2,1)}, u32[]{:S(2)}, u32[]{:S(2)}) collective-permute-start(bf16[128,2,128]{2,0,1:T(8,128)(2,1)} %fusion.70), channel_id=1, source_target_pairs={{0,60},{2,62},{4,0},{6,2},{8,4},{10,6},{12,8},{14,10},{16,12},{18,... | collective-permute-start | bytes 196616 | tf_op jit(solution)/shard_map/ppermute | solution.py:17
  132.8 2.1 %all_to_all.143 = bf16[2,64,2048]{2,1,0:T(8,128)(2,1)} reshape(bf16[128,2,8,128]{3,2,1,0:T(8,128)(2,1)} %copy.207) | data formatting | bytes 1048576 | tf_op jit(solution)/shard_map/all_to_all | solution.py:200
  134.8 4.2 %all-to-all-start.3 = ((bf16[2,64,2048]{2,1,0:T(8,128)(2,1)}), bf16[2,64,2048]{2,1,0:T(8,128)(2,1)}, u32[]{:S(2)}, u32[]{:S(2)}) async-start(bf16[2,64,2048]{2,1,0:T(8,128)(2,1)} %all_to_all.143), calls=%async_computation.3 | async-start | bytes 1048576 | tf_op jit(solution)/shard_map/all_to_all | solution.py:200
  142.0 2.8 %collective-permute-start.7 = (bf16[128,2,128]{2,0,1:T(8,128)(2,1)S(1)}, bf16[128,2,128]{2,0,1:T(8,128)(2,1)S(1)}, u32[]{:S(2)}, u32[]{:S(2)}) collective-permute-start(bf16[128,2,128]{2,0,1:T(8,128)(2,1)S(1)} %fusion.69), channel_id=1, source_target_pairs={{0,62},{2,0},{4,2},{6,4},{8,6},{10,8},{12,10},{14,12},{16,14},{18,... | collective-permute-start | bytes 196616 | tf_op jit(solution)/shard_map/ppermute | solution.py:17
  146.8 3.3 %all-to-all-start.10 = ((bf16[2,64,256]{2,1,0:T(8,128)(2,1)}), bf16[2,64,256]{2,1,0:T(8,128)(2,1)S(1)}, u32[]{:S(2)}, u32[]{:S(2)}) async-start(bf16[2,64,256]{2,1,0:T(8,128)(2,1)} %all_to_all.165), calls=%async_computation.10 | async-start | bytes 131072 | tf_op jit(solution)/shard_map/all_to_all | solution.py:217
  155.5 3.3 %all-to-all-start.9 = ((bf16[2,64,256]{2,1,0:T(8,128)(2,1)}), bf16[2,64,256]{2,1,0:T(8,128)(2,1)S(1)}, u32[]{:S(2)}, u32[]{:S(2)}) async-start(bf16[2,64,256]{2,1,0:T(8,128)(2,1)} %all_to_all.162), calls=%async_computation.9 | async-start | bytes 131072 | tf_op jit(solution)/shard_map/all_to_all | solution.py:210
  160.6 2.4 %all-to-all-done.9 = bf16[2,64,256]{2,1,0:T(8,128)(2,1)S(1)} async-done(((bf16[2,64,256]{2,1,0:T(8,128)(2,1)}), bf16[2,64,256]{2,1,0:T(8,128)(2,1)S(1)}, u32[]{:S(2)}, u32[]{:S(2)}) %all-to-all-start.9) | async-done | bytes 65568 | tf_op jit(solution)/shard_map/all_to_all | solution.py:210
  162.9 3.5 %all-to-all-start.8 = ((bf16[2,64,2048]{2,1,0:T(8,128)(2,1)}), bf16[2,64,2048]{2,1,0:T(8,128)(2,1)S(1)}, u32[]{:S(2)}, u32[]{:S(2)}) async-start(bf16[2,64,2048]{2,1,0:T(8,128)(2,1)} %all_to_all.159), calls=%async_computation.8 | async-start | bytes 1048576 | tf_op jit(solution)/shard_map/all_to_all | solution.py:203
  167.9 7.8 %all-to-all-done.8 = bf16[2,64,2048]{2,1,0:T(8,128)(2,1)S(1)} async-done(((bf16[2,64,2048]{2,1,0:T(8,128)(2,1)}), bf16[2,64,2048]{2,1,0:T(8,128)(2,1)S(1)}, u32[]{:S(2)}, u32[]{:S(2)}) %all-to-all-start.8) | async-done | bytes 524320 | tf_op jit(solution)/shard_map/all_to_all | solution.py:203
  (174 shorter events, 55.1 us)
Async XLA Ops:
  2.1 7.4 %all-to-all-start.4 = ((bf16[64,2,256]{2,0,1:T(8,128)(2,1)}), bf16[64,2,256]{2,0,1:T(8,128)(2,1)S(1)}, u32[]{:S(2)}, u32[]{:S(2)}) async-start(bf16[64,2,256]{2,0,1:T(8,128)(2,1)} %copy.209), calls=%async_computation.4 | async-start | bytes 131072 | tf_op jit(solution)/shard_map/all_to_all | solution.py:156
  6.3 6.6 %copy-start.26 = (s32[64]{0:T(128)S(1)}, s32[64]{0:T(128)}, u32[]{:S(2)}) copy-start(s32[64]{0:T(128)} %param.8) | copy-start | bytes 772
  6.3 6.7 %copy-start.24 = (bf16[1,64,512]{2,1,0:T(8,128)(2,1)S(1)}, bf16[1,64,512]{2,1,0:T(8,128)(2,1)}, u32[]{:S(2)}) copy-start(bf16[1,64,512]{2,1,0:T(8,128)(2,1)} %param.10) | copy-start | bytes 196612
  6.3 21.4 %copy-start.10 = (bf16[1,64,4096]{2,1,0:T(8,128)(2,1)S(1)}, bf16[1,64,4096]{2,1,0:T(8,128)(2,1)}, u32[]{:S(2)}) copy-start(bf16[1,64,4096]{2,1,0:T(8,128)(2,1)} %param.12) | copy-start | bytes 1572868
  9.5 7.4 %all-to-all-start.6 = ((bf16[64,2,256]{2,0,1:T(8,128)(2,1)}), bf16[64,2,256]{2,0,1:T(8,128)(2,1)S(1)}, u32[]{:S(2)}, u32[]{:S(2)}) async-start(bf16[64,2,256]{2,0,1:T(8,128)(2,1)} %copy.213), calls=%async_computation.6 | async-start | bytes 131072 | tf_op jit(solution)/shard_map/all_to_all | solution.py:157
  13.6 6.6 %copy-start.25 = (bf16[1,64,512]{2,1,0:T(8,128)(2,1)S(1)}, bf16[1,64,512]{2,1,0:T(8,128)(2,1)}, u32[]{:S(2)}) copy-start(bf16[1,64,512]{2,1,0:T(8,128)(2,1)} %param.11) | copy-start | bytes 196612
  17.0 7.4 %all-to-all-start = ((bf16[64,2,256]{2,0,1:T(8,128)(2,1)}), bf16[64,2,256]{2,0,1:T(8,128)(2,1)S(1)}, u32[]{:S(2)}, u32[]{:S(2)}) async-start(bf16[64,2,256]{2,0,1:T(8,128)(2,1)} %copy.186), calls=%async_computation | async-start | bytes 131072 | tf_op jit(solution)/shard_map/all_to_all | solution.py:153
  24.4 7.5 %all-to-all-start.2 = ((bf16[64,2,256]{2,0,1:T(8,128)(2,1)}), bf16[64,2,256]{2,0,1:T(8,128)(2,1)S(1)}, u32[]{:S(2)}, u32[]{:S(2)}) async-start(bf16[64,2,256]{2,0,1:T(8,128)(2,1)} %copy.190), calls=%async_computation.2 | async-start | bytes 131072 | tf_op jit(solution)/shard_map/all_to_all | solution.py:154
  31.9 11.0 %all-to-all-start.5 = ((bf16[64,2,2048]{2,0,1:T(8,128)(2,1)}), bf16[64,2,2048]{2,0,1:T(8,128)(2,1)S(1)}, u32[]{:S(2)}, u32[]{:S(2)}) async-start(bf16[64,2,2048]{2,0,1:T(8,128)(2,1)} %copy.210), calls=%async_computation.5 | async-start | bytes 1048576 | tf_op jit(solution)/shard_map/all_to_all | solution.py:155
  35.5 17.1 %collective-permute-start.4 = (bf16[128,2,2,128]{3,0,2,1:T(8,128)(2,1)S(1)}, bf16[128,2,2,128]{3,0,2,1:T(8,128)(2,1)S(1)}, u32[]{:S(2)}, u32[]{:S(2)}) collective-permute-start(bf16[128,2,2,128]{3,0,2,1:T(8,128)(2,1)S(1)} %pad_maximum_fusion.1), channel_id=1, source_target_pairs={{0,2},{2,4},{4,6},{6,8},{8,10},{10,12},{12,14},{14,16},{16,18},{18... | collective-permute-start | bytes 393224 | tf_op jit(solution)/shard_map/ppermute | solution.py:17
  42.9 21.9 %all-to-all-start.1 = ((bf16[64,2,2048]{2,0,1:T(8,128)(2,1)}), bf16[64,2,2048]{2,0,1:T(8,128)(2,1)S(1)}, u32[]{:S(2)}, u32[]{:S(2)}) async-start(bf16[64,2,2048]{2,0,1:T(8,128)(2,1)} %copy.187), calls=%async_computation.1 | async-start | bytes 1048576 | tf_op jit(solution)/shard_map/all_to_all | solution.py:152
  46.4 16.4 %collective-permute-start = (bf16[128,2,2,128]{3,0,2,1:T(8,128)(2,1)S(1)}, bf16[128,2,2,128]{3,0,2,1:T(8,128)(2,1)}, u32[]{:S(2)}, u32[]{:S(2)}) collective-permute-start(bf16[128,2,2,128]{3,0,2,1:T(8,128)(2,1)S(1)} %pad_maximum_fusion), channel_id=1, source_target_pairs={{0,2},{2,4},{4,6},{6,8},{8,10},{10,12},{12,14},{14,16},{16,18},{18... | collective-permute-start | bytes 393224 | tf_op jit(solution)/shard_map/ppermute | solution.py:17
  52.6 26.5 %collective-permute-start.5 = (bf16[128,2,2,128]{3,0,2,1:T(8,128)(2,1)S(1)}, bf16[128,2,2,128]{3,0,2,1:T(8,128)(2,1)S(1)}, u32[]{:S(2)}, u32[]{:S(2)}) collective-permute-start(bf16[128,2,2,128]{3,0,2,1:T(8,128)(2,1)S(1)} %collective-permute-done.4), channel_id=1, source_target_pairs={{0,2},{2,4},{4,6},{6,8},{8,10},{10,12},{12,14},{14,16},{16,18},{18... | collective-permute-start | bytes 393224 | tf_op jit(solution)/shard_map/ppermute | solution.py:17
  62.7 20.3 %collective-permute-start.1 = (bf16[128,2,2,128]{3,0,2,1:T(8,128)(2,1)}, bf16[128,2,2,128]{3,0,2,1:T(8,128)(2,1)}, u32[]{:S(2)}, u32[]{:S(2)}) collective-permute-start(bf16[128,2,2,128]{3,0,2,1:T(8,128)(2,1)} %collective-permute-done), channel_id=1, source_target_pairs={{0,2},{2,4},{4,6},{6,8},{8,10},{10,12},{12,14},{14,16},{16,18},{18... | collective-permute-start | bytes 393224 | tf_op jit(solution)/shard_map/ppermute | solution.py:17
  64.8 10.9 %all-to-all-start.7 = ((bf16[64,2,2048]{2,0,1:T(8,128)(2,1)}), bf16[64,2,2048]{2,0,1:T(8,128)(2,1)}, u32[]{:S(2)}, u32[]{:S(2)}) async-start(bf16[64,2,2048]{2,0,1:T(8,128)(2,1)} %copy.219), calls=%async_computation.7 | async-start | bytes 1048576 | tf_op jit(solution)/shard_map/all_to_all | solution.py:158
  71.7 18.2 %copy-start.21 = (f32[2,8,128]{2,1,0:T(8,128)}, f32[2,8,128]{2,1,0:T(8,128)S(1)}, u32[]{:S(2)}) copy-start(f32[2,8,128]{2,1,0:T(8,128)S(1)} %get-tuple-element.43) | copy-start | bytes 24580
  79.1 10.5 %collective-permute-start.6 = (bf16[128,2,2,128]{3,0,2,1:T(8,128)(2,1)S(1)}, bf16[128,2,2,128]{3,0,2,1:T(8,128)(2,1)S(1)}, u32[]{:S(2)}, u32[]{:S(2)}) collective-permute-start(bf16[128,2,2,128]{3,0,2,1:T(8,128)(2,1)S(1)} %collective-permute-done.5), channel_id=1, source_target_pairs={{0,2},{2,4},{4,6},{6,8},{8,10},{10,12},{12,14},{14,16},{16,18},{18... | collective-permute-start | bytes 393224 | tf_op jit(solution)/shard_map/ppermute | solution.py:17
  83.0 6.6 %copy-start.16 = (pred[128,128]{0,1:T(8,128)(4,1)S(1)}, pred[128,128]{0,1:T(8,128)(4,1)}, u32[]{:S(2)}) copy-start(pred[128,128]{0,1:T(8,128)(4,1)} %get-tuple-element.29) | copy-start | bytes 49156
  84.2 36.7 %collective-permute-start.2 = (bf16[128,2,2,128]{3,0,2,1:T(8,128)(2,1)}, bf16[128,2,2,128]{3,0,2,1:T(8,128)(2,1)S(1)}, u32[]{:S(2)}, u32[]{:S(2)}) collective-permute-start(bf16[128,2,2,128]{3,0,2,1:T(8,128)(2,1)} %collective-permute-done.1), channel_id=1, source_target_pairs={{0,2},{2,4},{4,6},{6,8},{8,10},{10,12},{12,14},{14,16},{16,18},{18... | collective-permute-start | bytes 393224 | tf_op jit(solution)/shard_map/ppermute | solution.py:17
  89.6 20.7 %copy-start.13 = (bf16[128,2,2,128]{3,0,2,1:T(8,128)(2,1)}, bf16[128,2,2,128]{3,0,2,1:T(8,128)(2,1)S(1)}, u32[]{:S(2)}) copy-start(bf16[128,2,2,128]{3,0,2,1:T(8,128)(2,1)S(1)} %collective-permute-done.6) | copy-start | bytes 393220
  93.5 48.5 %collective-permute-start.12 = (bf16[128,2,128]{2,0,1:T(8,128)(2,1)}, bf16[128,2,128]{2,0,1:T(8,128)(2,1)}, u32[]{:S(2)}, u32[]{:S(2)}) collective-permute-start(bf16[128,2,128]{2,0,1:T(8,128)(2,1)} %fusion.66), channel_id=1, source_target_pairs={{0,58},{2,60},{4,62},{6,0},{8,2},{10,4},{12,6},{14,8},{16,10},{18,... | collective-permute-start | bytes 196616 | tf_op jit(solution)/shard_map/ppermute | solution.py:17
  101.2 43.6 %collective-permute-start.11 = (bf16[128,2,128]{2,0,1:T(8,128)(2,1)}, bf16[128,2,128]{2,0,1:T(8,128)(2,1)}, u32[]{:S(2)}, u32[]{:S(2)}) collective-permute-start(bf16[128,2,128]{2,0,1:T(8,128)(2,1)} %fusion.67), channel_id=1, source_target_pairs={{0,60},{2,62},{4,0},{6,2},{8,4},{10,6},{12,8},{14,10},{16,12},{18,... | collective-permute-start | bytes 196616 | tf_op jit(solution)/shard_map/ppermute | solution.py:17
  105.8 39.0 %collective-permute-start.10 = (bf16[128,2,128]{2,0,1:T(8,128)(2,1)}, bf16[128,2,128]{2,0,1:T(8,128)(2,1)}, u32[]{:S(2)}, u32[]{:S(2)}) collective-permute-start(bf16[128,2,128]{2,0,1:T(8,128)(2,1)} %fusion.68), channel_id=1, source_target_pairs={{0,62},{2,0},{4,2},{6,4},{8,6},{10,8},{12,10},{14,12},{16,14},{18,... | collective-permute-start | bytes 196616 | tf_op jit(solution)/shard_map/ppermute | solution.py:17
  110.2 8.0 %copy-start.5 = (bf16[2,8,128,128]{2,3,1,0:T(8,128)(2,1)}, bf16[2,8,128,128]{2,3,1,0:T(8,128)(2,1)S(1)}, u32[]{:S(2)}) copy-start(bf16[2,8,128,128]{2,3,1,0:T(8,128)(2,1)S(1)} %fusion.52) | copy-start | bytes 1572868
  111.5 38.6 %collective-permute-start.9 = (bf16[128,2,128]{2,0,1:T(8,128)(2,1)}, bf16[128,2,128]{2,0,1:T(8,128)(2,1)}, u32[]{:S(2)}, u32[]{:S(2)}) collective-permute-start(bf16[128,2,128]{2,0,1:T(8,128)(2,1)} %fusion.71), channel_id=1, source_target_pairs={{0,58},{2,60},{4,62},{6,0},{8,2},{10,4},{12,6},{14,8},{16,10},{18,... | collective-permute-start | bytes 196616 | tf_op jit(solution)/shard_map/ppermute | solution.py:17
  120.9 29.2 %collective-permute-start.8 = (bf16[128,2,128]{2,0,1:T(8,128)(2,1)}, bf16[128,2,128]{2,0,1:T(8,128)(2,1)}, u32[]{:S(2)}, u32[]{:S(2)}) collective-permute-start(bf16[128,2,128]{2,0,1:T(8,128)(2,1)} %fusion.70), channel_id=1, source_target_pairs={{0,60},{2,62},{4,0},{6,2},{8,4},{10,6},{12,8},{14,10},{16,12},{18,... | collective-permute-start | bytes 196616 | tf_op jit(solution)/shard_map/ppermute | solution.py:17
  134.8 12.0 %all-to-all-start.3 = ((bf16[2,64,2048]{2,1,0:T(8,128)(2,1)}), bf16[2,64,2048]{2,1,0:T(8,128)(2,1)}, u32[]{:S(2)}, u32[]{:S(2)}) async-start(bf16[2,64,2048]{2,1,0:T(8,128)(2,1)} %all_to_all.143), calls=%async_computation.3 | async-start | bytes 1048576 | tf_op jit(solution)/shard_map/all_to_all | solution.py:200
  142.0 8.1 %collective-permute-start.7 = (bf16[128,2,128]{2,0,1:T(8,128)(2,1)S(1)}, bf16[128,2,128]{2,0,1:T(8,128)(2,1)S(1)}, u32[]{:S(2)}, u32[]{:S(2)}) collective-permute-start(bf16[128,2,128]{2,0,1:T(8,128)(2,1)S(1)} %fusion.69), channel_id=1, source_target_pairs={{0,62},{2,0},{4,2},{6,4},{8,6},{10,8},{12,10},{14,12},{16,14},{18,... | collective-permute-start | bytes 196616 | tf_op jit(solution)/shard_map/ppermute | solution.py:17
  146.8 8.7 %all-to-all-start.10 = ((bf16[2,64,256]{2,1,0:T(8,128)(2,1)}), bf16[2,64,256]{2,1,0:T(8,128)(2,1)S(1)}, u32[]{:S(2)}, u32[]{:S(2)}) async-start(bf16[2,64,256]{2,1,0:T(8,128)(2,1)} %all_to_all.165), calls=%async_computation.10 | async-start | bytes 131072 | tf_op jit(solution)/shard_map/all_to_all | solution.py:217
  153.4 24.1 %collective-permute-start.3 = (bf16[64,4096]{1,0:T(8,128)(2,1)S(1)}, bf16[64,4096]{1,0:T(8,128)(2,1)S(1)}, u32[]{:S(2)}, u32[]{:S(2)}) collective-permute-start(bf16[64,4096]{1,0:T(8,128)(2,1)S(1)} %bitcast.540), channel_id=1, source_target_pairs={{0,64},{64,128},{128,192},{192,256},{256,320},{320,384},{384,448},... | collective-permute-start | bytes 1572872 | tf_op jit(solution)/shard_map/ppermute | solution.py:23
  155.5 7.4 %all-to-all-start.9 = ((bf16[2,64,256]{2,1,0:T(8,128)(2,1)}), bf16[2,64,256]{2,1,0:T(8,128)(2,1)S(1)}, u32[]{:S(2)}, u32[]{:S(2)}) async-start(bf16[2,64,256]{2,1,0:T(8,128)(2,1)} %all_to_all.162), calls=%async_computation.9 | async-start | bytes 131072 | tf_op jit(solution)/shard_map/all_to_all | solution.py:210
  162.9 12.8 %all-to-all-start.8 = ((bf16[2,64,2048]{2,1,0:T(8,128)(2,1)}), bf16[2,64,2048]{2,1,0:T(8,128)(2,1)S(1)}, u32[]{:S(2)}, u32[]{:S(2)}) async-start(bf16[2,64,2048]{2,1,0:T(8,128)(2,1)} %all_to_all.159), calls=%async_computation.8 | async-start | bytes 1048576 | tf_op jit(solution)/shard_map/all_to_all | solution.py:203
  (19 other events, 40.3 us)
where the time goes:
time: 181 us; the launch traced here: 178 us
  starting transfers between devices  89.9 us (50%)
  waiting for transfers between devices  32.4 us (18%)
  local copies, waits for them, and re-layouts  27 us (15%)
  matrix products  25.1 us (14%)
  other arithmetic  2.31 us (1%)
    ppermute x12, starting transfers between devices, shifted(): return lax.ppermute(value, axis, pairs)  49.2 us
    ppermute x12, waiting for transfers between devices, shifted(): return lax.ppermute(value, axis, pairs)  9.48 us
    dot_general x8, matrix products, head_scores(): jnp.einsum('qgrd,kgd->grqk', query_rows, key_row_block, preferred_element...  8.19 us
    all_to_all x1, waiting for transfers between devices, group_plan(): lax.all_to_all(query_grad.astype(jnp.bfloat16).reshape(span_rows, -1), 'u...  7.85 us
    unnamed x58, local copies, waits for them, and re-layouts  6.65 us
    dot_general x8, matrix products, flash_update(): jnp.einsum('grqk,kgd->qgrd', raised.astype(jnp.bfloat16), kv_block[:, 1],...  5.56 us
    all_to_all x1, starting transfers between devices, group_plan(): lax.all_to_all(attention.reshape(span_rows, -1), 'uly', split_axis=0, con...  4.21 us
    all_to_all x1, starting transfers between devices, group_plan(): lax.all_to_all(out_grad[0], 'uly', split_axis=1, concat_axis=0, tiled=True)  4.21 us
  transfers between devices with their start and end apart: 24, of which 10 were waited for; matrix products, arithmetic and copies ran while one was open for 24% of the time, Pallas kernels for 0%

commit v1 on v0

v1 whole, which is shorter than its diff:
```python
import functools
import math

import jax
import jax.numpy as jnp
from jax import lax
from jax.experimental import pallas as pl
from jax.experimental.pallas import tpu as pltpu
from jax.sharding import PartitionSpec as P

HEAD = 128
GQA = 8
KVH = 4
TOK = 64
SLOTS_SEEN = 8
KEYS = SLOTS_SEEN * TOK
ROWS = GQA * TOK
WIDE = GQA * HEAD
NEG = -1e30
SCALE = HEAD ** -0.5
SCALE2 = SCALE * math.log2(math.e)
MESH = pl.DeviceIdType.MESH

NT = (((1,), (1,)), ((), ()))
NN = (((1,), (0,)), ((), ()))
TN = (((0,), (0,)), ((), ()))


def dot(a, b, dims):
    return lax.dot_general(a, b, dims, preferred_element_type=jnp.float32)


def kernel(
    order, qf_in, kf_in, vf_in, qb_in, kb_in, vb_in, do_in,
    handed_out, dq_out, dk_out, dv_out,
    kvf, kvb, qf, qb, do, att, dq, part, own, got, total, blank,
    in_sem, kv_sem, out_sem, g_send, g_recv, r_send, r_recv, h_send, h_recv,
):
    pipe, pipes = lax.axis_index("pipe"), lax.axis_size("pipe")
    blk, blks = lax.axis_index("blk"), lax.axis_size("blk")
    uly = lax.axis_index("uly")
    y_hi = lax.rem(blk, 2)
    z, planes = blk // 2, blks // 2
    even = y_hi == 0
    odd = y_hi == 1

    partner = {"uly": 1 - uly}
    cross = {"blk": blk + 1 - 2 * y_hi, "uly": 1 - uly}
    above = {"blk": lax.rem(blk + 2, blks)}
    below = {"blk": lax.rem(blk + blks - 2, blks)}
    after = {"pipe": lax.rem(pipe + 1, pipes)}
    before = {"pipe": lax.rem(pipe + pipes - 1, pipes)}

    barrier = pltpu.get_barrier_semaphore()
    for peer in (partner, cross, above, below, after, before):
        pl.semaphore_signal(barrier, inc=1, device_id=peer, device_id_type=MESH)

    loads = [
        pltpu.make_async_copy(kb_in, kvb.at[0, 0], kv_sem.at[0]),
        pltpu.make_async_copy(vb_in, kvb.at[0, 1], kv_sem.at[1]),
        pltpu.make_async_copy(kf_in, kvf.at[0, 0], kv_sem.at[2]),
        pltpu.make_async_copy(vf_in, kvf.at[0, 1], kv_sem.at[3]),
        pltpu.make_async_copy(qb_in, qb, in_sem.at[0]),
        pltpu.make_async_copy(do_in, do, in_sem.at[1]),
        pltpu.make_async_copy(qf_in, qf, in_sem.at[2]),
    ]
    for load in loads:
        load.start()

    target = {1: partner, 2: above, 3: cross, 4: partner, 5: cross, 6: above, 7: partner}
    back = {1: partner, 2: below, 3: cross, 4: partner, 5: cross, 6: below, 7: partner}

    def message(phase, r, c, source):
        kv = (kvb, kvf)[phase]
        return pltpu.make_async_remote_copy(
            src_ref=kv.at[source, c],
            dst_ref=kv.at[r, c],
            send_sem=g_send.at[phase, c, r],
            recv_sem=g_recv.at[phase, c, r],
            device_id=target[r],
            device_id_type=MESH,
        )

    def forward(phase, arrived, *sends):
        for c in range(2):
            if arrived:
                message(phase, arrived, c, 0).wait_recv()
            for r in sends:
                message(phase, r, c, arrived).start()

    def gather_own(phase):
        forward(phase, 0, 1, 2)

        @pl.when(even)
        def _():
            forward(phase, 0, 3)

    def gather_first(phase):
        @pl.when(even)
        def _():
            forward(phase, 2, 4, 5)
            forward(phase, 1)

        @pl.when(odd)
        def _():
            forward(phase, 2, 3)
            forward(phase, 1, 6)

    def gather_second(phase):
        @pl.when(even)
        def _():
            forward(phase, 3, 6)

        @pl.when(odd)
        def _():
            forward(phase, 3, 4)

    def gather_third(phase):
        @pl.when(even)
        def _():
            forward(phase, 6, 7)
            forward(phase, 4)
            forward(phase, 5)

        @pl.when(odd)
        def _():
            forward(phase, 6, 5)
            forward(phase, 5, 7)
            forward(phase, 4)

    def gather_last(phase):
        forward(phase, 7)

    def term(g, r):
        return pltpu.make_async_remote_copy(
            src_ref=part.at[g, r],
            dst_ref=got.at[g, r],
            send_sem=r_send.at[g, r],
            recv_sem=r_recv.at[g, r],
            device_id=back[r],
            device_id_type=MESH,
        )

    def take(g, r, into):
        term(g, r).wait_recv()
        part[g, into] = (
            part[g, into].astype(jnp.float32) + got[g, r].astype(jnp.float32)
        ).astype(jnp.bfloat16)

    def return_first(g):
        term(g, 7).start()
        term(g, 4).start()

        @pl.when(even)
        def _():
            term(g, 5).start()
            term(g, 1).start()

    def return_second(g):
        @pl.when(even)
        def _():
            take(g, 7, 6)
            term(g, 6).start()
            take(g, 4, 2)

        @pl.when(odd)
        def _():
            take(g, 7, 5)
            term(g, 5).start()
            take(g, 4, 3)
            term(g, 3).start()
            take(g, 5, 6)
            term(g, 6).start()

    def return_third(g):
        @pl.when(even)
        def _():
            take(g, 6, 3)
            term(g, 3).start()
            take(g, 5, 2)
            term(g, 2).start()

        @pl.when(odd)
        def _():
            take(g, 6, 1)
            term(g, 1).start()

    def return_fourth(g):
        @pl.when(odd)
        def _():
            take(g, 3, 2)
            term(g, 2).start()

    y = 2 * y_hi + uly
    col_p, col_x, col_d = 2 * y_hi + 1 - uly, 3 - y, 2 * (1 - y_hi) + uly
    plane = [4 * lax.rem(z + planes - k, planes) for k in range(3)]
    o = 1 - y_hi
    held = [
        plane[0] + y,
        plane[0] + col_p,
        plane[1] + y,
        o * plane[1] + y_hi * plane[0] + col_x,
        o * (plane[1] + col_p) + y_hi * (plane[0] + col_d),
        plane[1] + o * col_d + y_hi * col_x,
        o * (plane[2] + col_x) + y_hi * (plane[1] + col_p),
        o * plane[2] + y_hi * plane[1] + col_d,
    ]
    mine = order[held[0]]
    offsets = [None] + [jnp.where(order[held[r]] < mine, 0.0, NEG) for r in range(1, SLOTS_SEEN)]

    def stacked(ref, g):
        return jnp.concatenate(
            [ref[:, pl.ds(pl.multiple_of(g * WIDE + h * HEAD, HEAD), HEAD)] for h in range(GQA)], axis=0
        )

    def keys(ref, c, g):
        return ref[:, c, :, pl.ds(pl.multiple_of(g * HEAD, HEAD), HEAD)].reshape(KEYS, HEAD)

    def raised(k, q):
        raw = dot(k, q, NT) * SCALE2
        key = lax.broadcasted_iota(jnp.int32, (TOK, ROWS), 0)
        row = lax.broadcasted_iota(jnp.int32, (TOK, ROWS), 1) % TOK
        pieces = [jnp.where(key <= row, raw[:TOK], NEG)]
        for r in range(1, SLOTS_SEEN):
            pieces.append(raw[r * TOK:(r + 1) * TOK] + offsets[r])
        scores = jnp.concatenate(pieces, axis=0)
        p = jnp.exp2(scores - jnp.max(scores, axis=0, keepdims=True))
        return p, 1.0 / jnp.sum(p, axis=0, keepdims=True)

    def spread(ref, g, value):
        for h in range(GQA):
            ref[:, pl.ds(pl.multiple_of(g * WIDE + h * HEAD, HEAD), HEAD)] = value[h * TOK:(h + 1) * TOK]

    def columns(ref, g):
        return ref.at[:, pl.ds(pl.multiple_of(g * WIDE, WIDE), WIDE)]

    def grad_copy(g):
        return pltpu.make_async_copy(columns(dq, g), columns(dq_out, g), out_sem.at[g])

    def blank_copy(g):
        return pltpu.make_async_copy(blank, columns(handed_out, g), out_sem.at[KVH + g])

    def hand(g):
        return pltpu.make_async_remote_copy(
            src_ref=columns(att, g),
            dst_ref=columns(handed_out, g),
            send_sem=h_send.at[g],
            recv_sem=h_recv.at[g],
            device_id=after,
            device_id_type=MESH,
        )

    def backward(g):
        k, v = keys(kvb, 0, g), keys(kvb, 1, g)
        q, up = stacked(qb, g), stacked(do, g)
        p, inverse = raised(k, q)
        p = p * inverse
        dp = dot(v, up, NT)
        delta = jnp.sum(p * dp, axis=0, keepdims=True)
        ds = (p * (dp - delta)).astype(jnp.bfloat16)
        dv = dot(p.astype(jnp.bfloat16), up, NN)
        dk = dot(ds, q, NN) * SCALE
        own[g, 0] = dk[:TOK]
        own[g, 1] = dv[:TOK]
        part[g, :, 0] = dk.reshape(SLOTS_SEEN, TOK, HEAD).astype(jnp.bfloat16)
        part[g, :, 1] = dv.reshape(SLOTS_SEEN, TOK, HEAD).astype(jnp.bfloat16)
        grad = dot(k, ds, TN) * SCALE
        spread(dq, g, grad.T.astype(jnp.bfloat16))
        grad_copy(g).start()

    def forwards(g):
        k, v = keys(kvf, 0, g), keys(kvf, 1, g)
        p, inverse = raised(k, stacked(qf, g))
        weighted = dot(v, p.astype(jnp.bfloat16), TN) * inverse
        spread(att, g, weighted.T.astype(jnp.bfloat16))

        @pl.when(pipe < pipes - 1)
        def _():
            hand(g).start()

    loads[0].wait()
    loads[1].wait()
    pl.semaphore_wait(barrier, 6)
    gather_own(0)

    @pl.when(pipe == 0)
    def _():
        blank[...] = jnp.zeros_like(blank)
        for g in range(KVH):
            blank_copy(g).start()

    gather_first(0)
    gather_second(0)
    gather_third(0)
    loads[2].wait()
    loads[3].wait()
    gather_own(1)
    gather_last(0)
    loads[4].wait()
    loads[5].wait()
    loads[6].wait()

    def step(t, carry):
        @pl.when(t < KVH)
        def _():
            backward(t)
            return_first(t)

        @pl.when(t >= KVH)
        def _():
            forwards(t - KVH)

        @pl.when(t == 0)
        def _():
            gather_first(1)

        @pl.when(t == 1)
        def _():
            gather_second(1)

        @pl.when(t == 2)
        def _():
            gather_third(1)

        @pl.when(t == 3)
        def _():
            gather_last(1)

        @pl.when((t >= 1) & (t < KVH + 1))
        def _():
            return_second(t - 1)

        @pl.when((t >= 2) & (t < KVH + 2))
        def _():
            return_third(t - 2)

        @pl.when((t >= 3) & (t < KVH + 3))
        def _():
            return_fourth(t - 3)

        return carry

    lax.fori_loop(0, 2 * KVH, step, 0)

    for g in range(KVH):
        sums = own[g]
        for r in (1, 2):
            term(g, r).wait_recv()
            sums = sums + got[g, r].astype(jnp.float32)

        @pl.when(odd)
        def _():
            total[:, :, g * HEAD:(g + 1) * HEAD] = sums.astype(jnp.bfloat16)

        @pl.when(even)
        def _():
            term(g, 3).wait_recv()
            full = sums + got[g, 3].astype(jnp.float32)
            total[:, :, g * HEAD:(g + 1) * HEAD] = full.astype(jnp.bfloat16)

    stores = [
        pltpu.make_async_copy(total.at[0], dk_out, kv_sem.at[0]),
        pltpu.make_async_copy(total.at[1], dv_out, kv_sem.at[1]),
    ]
    for store in stores:
        store.start()
    for g in range(KVH):
        grad_copy(g).wait()
        for r in range(1, SLOTS_SEEN):
            term(g, r).wait_send()
    for phase in range(2):
        for c in range(2):
            for r in range(1, SLOTS_SEEN):
                message(phase, r, c, 0).wait_send()

    @pl.when(pipe < pipes - 1)
    def _():
        for g in range(KVH):
            hand(g).wait_send()

    @pl.when(pipe > 0)
    def _():
        for g in range(KVH):
            hand(g).wait_recv()

    @pl.when(pipe == 0)
    def _():
        for g in range(KVH):
            blank_copy(g).wait()

    for store in stores:
        store.wait()


def local(order, *arrays):
    bf16 = jnp.bfloat16
    wide, narrow = (TOK, KVH * WIDE), (TOK, KVH * HEAD)
    anywhere = pl.BlockSpec(memory_space=pl.ANY)
    dma = pltpu.SemaphoreType.DMA
    outs = pl.pallas_call(
        kernel,
        out_shape=[jax.ShapeDtypeStruct(s, bf16) for s in (wide, wide, narrow, narrow)],
        in_specs=[pl.BlockSpec(memory_space=pltpu.SMEM)] + [anywhere] * 7,
        out_specs=[anywhere] * 4,
        scratch_shapes=[
            pltpu.VMEM((SLOTS_SEEN, 2) + narrow, bf16),
            pltpu.VMEM((SLOTS_SEEN, 2) + narrow, bf16),
            pltpu.VMEM(wide, bf16),
            pltpu.VMEM(wide, bf16),
            pltpu.VMEM(wide, bf16),
            pltpu.VMEM(wide, bf16),
            pltpu.VMEM(wide, bf16),
            pltpu.VMEM((KVH, SLOTS_SEEN, 2, TOK, HEAD), bf16),
            pltpu.VMEM((KVH, 2, TOK, HEAD), jnp.float32),
            pltpu.VMEM((KVH, SLOTS_SEEN, 2, TOK, HEAD), bf16),
            pltpu.VMEM((2,) + narrow, bf16),
            pltpu.VMEM((TOK, WIDE), bf16),
            dma((3,)),
            dma((4,)),
            dma((2 * KVH,)),
            dma((2, 2, SLOTS_SEEN)),
            dma((2, 2, SLOTS_SEEN)),
            dma((KVH, SLOTS_SEEN)),
            dma((KVH, SLOTS_SEEN)),
            dma((KVH,)),
            dma((KVH,)),
        ],
        compiler_params=pltpu.CompilerParams(
            collective_id=0, has_side_effects=True, vmem_limit_bytes=40 * 1024 * 1024
        ),
    )(order, *[a[0] for a in arrays])
    return tuple(out[None] for out in outs)


def solution(mesh):
    split = P("pipe", ("blk", "uly"), None)
    return jax.shard_map(
        local,
        mesh=mesh,
        in_specs=(P(),) + (split,) * 7,
        out_specs=(split,) * 4,
        check_vma=False,
    )
```

time: 181 us -> 64.4 us (0.36)
  the two profiles are of different devices: /device:TPU:2 before, /device:TPU:29 now
where the time goes in v1:
time: 64.4 us; the launch traced here: 64 us
  Pallas kernels  53.3 us (83%)
  local copies, waits for them, and re-layouts  9.97 us (15%)
  between operations  0.66 us (1%)
    pallas_call x1, Pallas kernels, local(): pl.pallas_call(kernel, out_shape=[jax.ShapeDtypeStruct(s, bf16) for s in...  53.3 us
    unnamed x20, local copies, waits for them, and re-layouts  9.97 us

profile of v1, /device:TPU:29, one launch (start us, length us, event | category | flops | bytes accessed | tf_op | source)
XLA Modules:
  0.0 64.0 jit_solution(1905666842342929913)
XLA Ops:
  0.6 0.0 copy-start.7
  0.6 0.6 %copy-done.7 = s32[64]{0:T(128)S(1)} copy-done((s32[64]{0:T(128)S(1)}, s32[64]{0:T(128)}, u32[]{:S(2)}) %copy-start.7) | copy-done | bytes 280
  1.3 0.0 copy-start
  1.3 1.0 %copy-done = bf16[1,64,4096]{2,1,0:T(8,128)(2,1)S(1)} copy-done((bf16[1,64,4096]{2,1,0:T(8,128)(2,1)S(1)}, bf16[1,64,4096]{2,1,0:T(8,128)(2,1)}, u32[]{:S(2)}) %copy-start) | copy-done | bytes 524312
  2.3 0.0 copy-start.1
  2.3 1.0 %copy-done.1 = bf16[1,64,4096]{2,1,0:T(8,128)(2,1)S(1)} copy-done((bf16[1,64,4096]{2,1,0:T(8,128)(2,1)S(1)}, bf16[1,64,4096]{2,1,0:T(8,128)(2,1)}, u32[]{:S(2)}) %copy-start.1) | copy-done | bytes 524312
  3.4 0.0 copy-start.2
  3.4 1.0 %copy-done.2 = bf16[1,64,4096]{2,1,0:T(8,128)(2,1)S(1)} copy-done((bf16[1,64,4096]{2,1,0:T(8,128)(2,1)S(1)}, bf16[1,64,4096]{2,1,0:T(8,128)(2,1)}, u32[]{:S(2)}) %copy-start.2) | copy-done | bytes 524312
  4.4 0.0 copy-start.3
  4.4 0.8 %copy-done.3 = bf16[1,64,512]{2,1,0:T(8,128)(2,1)S(1)} copy-done((bf16[1,64,512]{2,1,0:T(8,128)(2,1)S(1)}, bf16[1,64,512]{2,1,0:T(8,128)(2,1)}, u32[]{:S(2)}) %copy-start.3) | copy-done | bytes 65560
  5.3 0.0 copy-start.4
  5.3 0.8 %copy-done.4 = bf16[1,64,512]{2,1,0:T(8,128)(2,1)S(1)} copy-done((bf16[1,64,512]{2,1,0:T(8,128)(2,1)S(1)}, bf16[1,64,512]{2,1,0:T(8,128)(2,1)}, u32[]{:S(2)}) %copy-start.4) | copy-done | bytes 65560
  6.1 0.0 copy-start.5
  6.1 0.8 %copy-done.5 = bf16[1,64,512]{2,1,0:T(8,128)(2,1)S(1)} copy-done((bf16[1,64,512]{2,1,0:T(8,128)(2,1)S(1)}, bf16[1,64,512]{2,1,0:T(8,128)(2,1)}, u32[]{:S(2)}) %copy-start.5) | copy-done | bytes 65560
  6.9 0.0 copy-start.6
  6.9 0.8 %copy-done.6 = bf16[1,64,512]{2,1,0:T(8,128)(2,1)S(1)} copy-done((bf16[1,64,512]{2,1,0:T(8,128)(2,1)S(1)}, bf16[1,64,512]{2,1,0:T(8,128)(2,1)}, u32[]{:S(2)}) %copy-start.6) | copy-done | bytes 65560
  7.8 53.3 %shard_map.111 = (bf16[64,4096]{1,0:T(8,128)(2,1)S(1)}, bf16[64,4096]{1,0:T(8,128)(2,1)S(1)}, bf16[64,512]{1,0:T(8,128)(2,1)S(1)}, bf16[64,512]{1,0:T(8,128)(2,1)S(1)}) custom-call(s32[64]{0:T(128)S(1)} %copy-done.7, bf16[64,4096]{1,0:T(8,128)(2,1)S(1)} %bitcast.13, bf16[64,512]{1,0:T(8,128)(2,1)S(1)} %bitcast.16, bf16[64,512]{1,0:T(8,128)(2,1)S(1)} %bitcast.17, ...), custom_call_target="tpu_custom_call" | custom-call | tf_op jit(solution)/shard_map/pallas_call | solution.py:400
  61.1 0.8 %copy.16 = bf16[1,64,4096]{2,1,0:T(8,128)(2,1)} copy(bf16[1,64,4096]{2,1,0:T(8,128)(2,1)S(1)} %bitcast.12) | data formatting | bytes 1048576
  61.9 0.8 %copy.17 = bf16[1,64,4096]{2,1,0:T(8,128)(2,1)} copy(bf16[1,64,4096]{2,1,0:T(8,128)(2,1)S(1)} %bitcast.11) | data formatting | bytes 1048576
  62.7 0.6 copy.18
  63.3 0.6 copy.19
Async XLA Ops:
  0.6 0.7 %copy-start.7 = (s32[64]{0:T(128)S(1)}, s32[64]{0:T(128)}, u32[]{:S(2)}) copy-start(s32[64]{0:T(128)} %order.1) | copy-start | bytes 772
  1.3 1.0 %copy-start = (bf16[1,64,4096]{2,1,0:T(8,128)(2,1)S(1)}, bf16[1,64,4096]{2,1,0:T(8,128)(2,1)}, u32[]{:S(2)}) copy-start(bf16[1,64,4096]{2,1,0:T(8,128)(2,1)} %param.9) | copy-start | bytes 1572868
  2.3 1.0 %copy-start.1 = (bf16[1,64,4096]{2,1,0:T(8,128)(2,1)S(1)}, bf16[1,64,4096]{2,1,0:T(8,128)(2,1)}, u32[]{:S(2)}) copy-start(bf16[1,64,4096]{2,1,0:T(8,128)(2,1)} %param.12) | copy-start | bytes 1572868
  3.4 1.0 %copy-start.2 = (bf16[1,64,4096]{2,1,0:T(8,128)(2,1)S(1)}, bf16[1,64,4096]{2,1,0:T(8,128)(2,1)}, u32[]{:S(2)}) copy-start(bf16[1,64,4096]{2,1,0:T(8,128)(2,1)} %param.15) | copy-start | bytes 1572868
  4.4 0.8 %copy-start.3 = (bf16[1,64,512]{2,1,0:T(8,128)(2,1)S(1)}, bf16[1,64,512]{2,1,0:T(8,128)(2,1)}, u32[]{:S(2)}) copy-start(bf16[1,64,512]{2,1,0:T(8,128)(2,1)} %param.10) | copy-start | bytes 196612
  5.3 0.8 %copy-start.4 = (bf16[1,64,512]{2,1,0:T(8,128)(2,1)S(1)}, bf16[1,64,512]{2,1,0:T(8,128)(2,1)}, u32[]{:S(2)}) copy-start(bf16[1,64,512]{2,1,0:T(8,128)(2,1)} %param.11) | copy-start | bytes 196612
  6.1 0.8 %copy-start.5 = (bf16[1,64,512]{2,1,0:T(8,128)(2,1)S(1)}, bf16[1,64,512]{2,1,0:T(8,128)(2,1)}, u32[]{:S(2)}) copy-start(bf16[1,64,512]{2,1,0:T(8,128)(2,1)} %param.13) | copy-start | bytes 196612
  6.9 0.8 %copy-start.6 = (bf16[1,64,512]{2,1,0:T(8,128)(2,1)S(1)}, bf16[1,64,512]{2,1,0:T(8,128)(2,1)}, u32[]{:S(2)}) copy-start(bf16[1,64,512]{2,1,0:T(8,128)(2,1)} %param.14) | copy-start | bytes 196612

commit v2 on v1

--- a/solution.py
+++ b/solution.py
@@ -19,6 +19,37 @@
 NEG = -1e30
 SCALE = HEAD ** -0.5
 SCALE2 = SCALE * math.log2(math.e)
+VMEM_BYTES = 60 * 1024 * 1024
+UNITS = ((0, 0, 1), (0, 1, 1), (0, 2, 1), (0, 3, 1), (1, 0, 2), (1, 2, 2))
+PAIRED = ((0, 0, 1), (0, 2, 1), )
+RETURNS = ("r1", "t7", "t6", "t45", "t5", "t3", "t4")
+EVEN = (
+    (("own", 3), ("own", 2), ("own", 0), ("own", 1), ("own", 5), ("f2", 2), ("f2", 0), ("f3", 0), ("own", 4),
+     ("f3", 2), ("f2", 1), ("f7", 0), ("f3", 1), ("f2", 3), ("f7", 1), ("f7", 2), ("f2", 5), ("f3", 3), ("f2", 4),
+     ("last", 0),),
+    (("f7", 3), ("r1", 0), ("last", 1),),
+    (("r1", 1), ("last", 2), ("f3", 4),),
+    (("t7", 0), ("t6", 0), ("f7", 4), ("r1", 2), ("last", 3),),
+    (("r1", 3), ("t7", 1), ("f3", 5), ("t7", 2), ("t6", 1), ("t45", 1), ("f7", 5), ("last", 4),),
+    (("t7", 3), ("t6", 2),),
+    (("last", 5), ("t45", 0), ("t6", 3),),
+    (("t45", 3), ("t45", 2),),
+    (),
+)
+ODD = (
+    (("own", 0), ("own", 1), ("own", 2), ("own", 3), ("own", 4), ("f2", 0), ("f1", 1), ("f2", 1), ("f1", 0),
+     ("f3", 0), ("f2", 2), ("f1", 3), ("own", 5), ("f1", 2), ("f2", 3), ("f3", 1), ("f6", 1), ("f7", 0), ("f6", 0),
+     ("f1", 4), ("f3", 3), ("f6", 3), ("f7", 1), ("f1", 5), ("f3", 2), ("f2", 4), ("last", 0), ("f3", 4), ("f7", 2),
+     ("f6", 2),),
+    (("f6", 4), ("f7", 3), ("f2", 5), ("last", 1),),
+    (("f3", 5), ("r1", 1), ("f6", 5), ("f7", 4), ("last", 2), ("r1", 0),),
+    (("r1", 2), ("last", 3),),
+    (("t7", 0), ("r1", 3), ("t7", 2), ("t3", 0), ("last", 4), ("t5", 0), ("f7", 5),),
+    (("t4", 0), ("t5", 1), ("t7", 1), ("t7", 3), ("t5", 2),),
+    (("t4", 2), ("t6", 0), ("last", 5), ("t5", 3), ("t3", 1),),
+    (("t3", 2), ("t6", 2), ("t4", 1), ("t6", 1),),
+    (("t4", 3), ("t3", 3), ("t6", 3),),
+)
 MESH = pl.DeviceIdType.MESH
 
 NT = (((1,), (1,)), ((), ()))
@@ -55,81 +86,60 @@
     for peer in (partner, cross, above, below, after, before):
         pl.semaphore_signal(barrier, inc=1, device_id=peer, device_id_type=MESH)
 
+    kv_loads = {}
+    for phase, sources in enumerate(((kb_in, vb_in), (kf_in, vf_in))):
+        for g in range(KVH):
+            kv_loads[phase, g] = [
+                pltpu.make_async_copy(
+                    source.at[:, g * HEAD:(g + 1) * HEAD], (kvb, kvf)[phase].at[0, g, c], kv_sem.at[phase, g, c]
+                )
+                for c, source in enumerate(sources)
+            ]
     loads = [
-        pltpu.make_async_copy(kb_in, kvb.at[0, 0], kv_sem.at[0]),
-        pltpu.make_async_copy(vb_in, kvb.at[0, 1], kv_sem.at[1]),
-        pltpu.make_async_copy(kf_in, kvf.at[0, 0], kv_sem.at[2]),
-        pltpu.make_async_copy(vf_in, kvf.at[0, 1], kv_sem.at[3]),
         pltpu.make_async_copy(qb_in, qb, in_sem.at[0]),
         pltpu.make_async_copy(do_in, do, in_sem.at[1]),
         pltpu.make_async_copy(qf_in, qf, in_sem.at[2]),
     ]
+    for pair in kv_loads.values():
+        for load in pair:
+            load.start()
     for load in loads:
         load.start()
 
-    target = {1: partner, 2: above, 3: cross, 4: partner, 5: cross, 6: above, 7: partner}
-    back = {1: partner, 2: below, 3: cross, 4: partner, 5: cross, 6: below, 7: partner}
-
-    def message(phase, r, c, source):
+    target = {1: partner, 2: above, 3: cross, 4: partner, 5: cross, 6: above, 7: above}
+    back = {1: partner, 2: below, 3: cross, 4: partner, 5: cross, 6: below, 7: below}
+
+    def paired(unit):
+        return unit in PAIRED
+
+    def message(unit, r, source):
+        phase, head, count = unit
         kv = (kvb, kvf)[phase]
         return pltpu.make_async_remote_copy(
-            src_ref=kv.at[source, c],
-            dst_ref=kv.at[r, c],
-            send_sem=g_send.at[phase, c, r],
-            recv_sem=g_recv.at[phase, c, r],
-            device_id=target[r],
+            src_ref=kv.at[source, pl.ds(head, count)],
+            dst_ref=kv.at[r, pl.ds(head, count)],
+            send_sem=g_send.at[phase, head, r],
+            recv_sem=g_recv.at[phase, head, r],
+            device_id=partner if r == 7 and paired(unit) else target[r],
             device_id_type=MESH,
         )
 
-    def forward(phase, arrived, *sends):
-        for c in range(2):
-            if arrived:
-                message(phase, arrived, c, 0).wait_recv()
-            for r in sends:
-                message(phase, r, c, arrived).start()
-
-    def gather_own(phase):
-        forward(phase, 0, 1, 2)
-
-        @pl.when(even)
-        def _():
-            forward(phase, 0, 3)
-
-    def gather_first(phase):
-        @pl.when(even)
-        def _():
-            forward(phase, 2, 4, 5)
-            forward(phase, 1)
-
-        @pl.when(odd)
-        def _():
-            forward(phase, 2, 3)
-            forward(phase, 1, 6)
-
-    def gather_second(phase):
-        @pl.when(even)
-        def _():
-            forward(phase, 3, 6)
-
-        @pl.when(odd)
-        def _():
-            forward(phase, 3, 4)
-
-    def gather_third(phase):
-        @pl.when(even)
-        def _():
-            forward(phase, 6, 7)
-            forward(phase, 4)
-            forward(phase, 5)
-
-        @pl.when(odd)
-        def _():
-            forward(phase, 6, 5)
-            forward(phase, 5, 7)
-            forward(phase, 4)
-
-    def gather_last(phase):
-        forward(phase, 7)
+    def forward(unit, arrived, *sends):
+        if arrived:
+            message(unit, arrived, 0).wait_recv()
+        for r in sends:
+            message(unit, r, arrived).start()
+
+    def own_slot(unit, *sends):
+        phase, head, count = unit
+        for g in range(head, head + count):
+            for load in kv_loads[phase, g]:
+                load.wait()
+        forward(unit, 0, *sends)
+
+    def last_slots(unit, *slots):
+        for r in slots:
+            forward(unit, r)
 
     def term(g, r):
         return pltpu.make_async_remote_copy(
@@ -147,49 +157,48 @@
             part[g, into].astype(jnp.float32) + got[g, r].astype(jnp.float32)
         ).astype(jnp.bfloat16)
 
-    def return_first(g):
-        term(g, 7).start()
-        term(g, 4).start()
-
-        @pl.when(even)
-        def _():
-            term(g, 5).start()
-            term(g, 1).start()
-
-    def return_second(g):
-        @pl.when(even)
-        def _():
-            take(g, 7, 6)
-            term(g, 6).start()
-            take(g, 4, 2)
-
-        @pl.when(odd)
-        def _():
-            take(g, 7, 5)
-            term(g, 5).start()
-            take(g, 4, 3)
-            term(g, 3).start()
-            take(g, 5, 6)
-            term(g, 6).start()
-
-    def return_third(g):
-        @pl.when(even)
-        def _():
-            take(g, 6, 3)
-            term(g, 3).start()
-            take(g, 5, 2)
-            term(g, 2).start()
-
-        @pl.when(odd)
-        def _():
-            take(g, 6, 1)
-            term(g, 1).start()
-
-    def return_fourth(g):
-        @pl.when(odd)
-        def _():
-            take(g, 3, 2)
-            term(g, 2).start()
+    def gather_moves(unit):
+        pair = paired(unit)
+        return {
+            "own": (lambda: own_slot(unit, 3, 2, 1), lambda: own_slot(unit, 2, 1)),
+            "f1": (None, lambda: forward(unit, 1, 6)),
+            "f2": (lambda: forward(unit, 2, 5, 4), lambda: forward(unit, 2, 3)),
+            "f3": (lambda: forward(unit, 3, 6), lambda: forward(unit, 3, 4)),
+            "f6": (None, lambda: forward(unit, 6, 5)),
+            "f7": (lambda: forward(unit, 6 if pair else 5, 7), lambda: forward(unit, 5 if pair else 4, 7)),
+            "last": (
+                lambda: last_slots(unit, 1, 4, 5 if pair else 6, 7),
+                lambda: last_slots(unit, 4 if pair else 5, 7),
+            ),
+        }
+
+    def back_send(g, *slots):
+        for r in slots:
+            term(g, r).start()
+
+    def back_sum(g, into, *slots):
+        for r in slots:
+            take(g, r, into)
+        term(g, into).start()
+
+    def return_moves(g):
+        return {
+            "r1": (lambda: back_send(g, 7, 4, 6, 1), lambda: back_send(g, 5, 7)),
+            "t7": (lambda: back_sum(g, 5, 7), lambda: back_sum(g, 4, 7)),
+            "t6": (lambda: back_sum(g, 3, 6), lambda: back_sum(g, 1, 6)),
+            "t45": (lambda: back_sum(g, 2, 4, 5), None),
+            "t5": (None, lambda: back_sum(g, 6, 5)),
+            "t3": (None, lambda: back_sum(g, 2, 3)),
+            "t4": (None, lambda: back_sum(g, 3, 4)),
+        }
+
+    def run(k):
+        for parity, table in enumerate((EVEN, ODD)):
+            @pl.when(y_hi == parity)
+            def _():
+                for name, index in table[k]:
+                    moves = return_moves(index) if name in RETURNS else gather_moves(UNITS[index])
+                    moves[name][parity]()
 
     y = 2 * y_hi + uly
     col_p, col_x, col_d = 2 * y_hi + 1 - uly, 3 - y, 2 * (1 - y_hi) + uly
@@ -214,7 +223,7 @@
         )
 
     def keys(ref, c, g):
-        return ref[:, c, :, pl.ds(pl.multiple_of(g * HEAD, HEAD), HEAD)].reshape(KEYS, HEAD)
+        return ref[:, g, c].reshape(KEYS, HEAD)
 
     def raised(k, q):
         raw = dot(k, q, NT) * SCALE2
@@ -278,10 +287,10 @@
         def _():
             hand(g).start()
 
-    loads[0].wait()
-    loads[1].wait()
     pl.semaphore_wait(barrier, 6)
-    gather_own(0)
+    run(0)
+    for load in loads:
+        load.wait()
 
     @pl.when(pipe == 0)
     def _():
@@ -289,54 +298,19 @@
         for g in range(KVH):
             blank_copy(g).start()
 
-    gather_first(0)
-    gather_second(0)
-    gather_third(0)
-    loads[2].wait()
-    loads[3].wait()
-    gather_own(1)
-    gather_last(0)
-    loads[4].wait()
-    loads[5].wait()
-    loads[6].wait()
-
     def step(t, carry):
         @pl.when(t < KVH)
         def _():
             backward(t)
-            return_first(t)
 
         @pl.when(t >= KVH)
         def _():
             forwards(t - KVH)
 
-        @pl.when(t == 0)
-        def _():
-            gather_first(1)
-
-        @pl.when(t == 1)
-        def _():
-            gather_second(1)
-
-        @pl.when(t == 2)
-        def _():
-            gather_third(1)
-
-        @pl.when(t == 3)
-        def _():
-            gather_last(1)
-
-        @pl.when((t >= 1) & (t < KVH + 1))
-        def _():
-            return_second(t - 1)
-
-        @pl.when((t >= 2) & (t < KVH + 2))
-        def _():
-            return_third(t - 2)
-
-        @pl.when((t >= 3) & (t < KVH + 3))
-        def _():
-            return_fourth(t - 3)
+        for k in range(2 * KVH):
+            @pl.when(t == k)
+            def _():
+                run(k + 1)
 
         return carry
 
@@ -359,8 +333,8 @@
             total[:, :, g * HEAD:(g + 1) * HEAD] = full.astype(jnp.bfloat16)
 
     stores = [
-        pltpu.make_async_copy(total.at[0], dk_out, kv_sem.at[0]),
-        pltpu.make_async_copy(total.at[1], dv_out, kv_sem.at[1]),
+        pltpu.make_async_copy(total.at[0], dk_out, out_sem.at[2 * KVH]),
+        pltpu.make_async_copy(total.at[1], dv_out, out_sem.at[2 * KVH + 1]),
     ]
     for store in stores:
         store.start()
@@ -368,10 +342,9 @@
         grad_copy(g).wait()
         for r in range(1, SLOTS_SEEN):
             term(g, r).wait_send()
-    for phase in range(2):
-        for c in range(2):
-            for r in range(1, SLOTS_SEEN):
-                message(phase, r, c, 0).wait_send()
+    for unit in UNITS:
+        for r in range(1, SLOTS_SEEN):
+            message(unit, r, 0).wait_send()
 
     @pl.when(pipe < pipes - 1)
     def _():
@@ -392,19 +365,33 @@
         store.wait()
 
 
+def settle(*refs):
+    ins, outs, held, sems = refs[:4], refs[4:8], refs[8:12], refs[12]
+    fetched = [pltpu.make_async_copy(ins[i], held[i], sems.at[0, i]) for i in range(4)]
+    stored = [pltpu.make_async_copy(held[i], outs[i], sems.at[1, i]) for i in range(4)]
+    for copy in fetched:
+        copy.start()
+    for fetch, store in zip(fetched, stored):
+        fetch.wait()
+        store.start()
+    for copy in stored:
+        copy.wait()
+
+
 def local(order, *arrays):
     bf16 = jnp.bfloat16
     wide, narrow = (TOK, KVH * WIDE), (TOK, KVH * HEAD)
     anywhere = pl.BlockSpec(memory_space=pl.ANY)
+    in_hbm = pl.BlockSpec(memory_space=pltpu.HBM)
     dma = pltpu.SemaphoreType.DMA
     outs = pl.pallas_call(
         kernel,
         out_shape=[jax.ShapeDtypeStruct(s, bf16) for s in (wide, wide, narrow, narrow)],
-        in_specs=[pl.BlockSpec(memory_space=pltpu.SMEM)] + [anywhere] * 7,
+        in_specs=[pl.BlockSpec(memory_space=pltpu.SMEM)] + [in_hbm] * 7,
         out_specs=[anywhere] * 4,
         scratch_shapes=[
-            pltpu.VMEM((SLOTS_SEEN, 2) + narrow, bf16),
-            pltpu.VMEM((SLOTS_SEEN, 2) + narrow, bf16),
+            pltpu.VMEM((SLOTS_SEEN, KVH, 2, TOK, HEAD), bf16),
+            pltpu.VMEM((SLOTS_SEEN, KVH, 2, TOK, HEAD), bf16),
             pltpu.VMEM(wide, bf16),
             pltpu.VMEM(wide, bf16),
             pltpu.VMEM(wide, bf16),
@@ -416,19 +403,27 @@
             pltpu.VMEM((2,) + narrow, bf16),
             pltpu.VMEM((TOK, WIDE), bf16),
             dma((3,)),
-            dma((4,)),
-            dma((2 * KVH,)),
-            dma((2, 2, SLOTS_SEEN)),
-            dma((2, 2, SLOTS_SEEN)),
+            dma((2, KVH, 2)),
+            dma((2 * KVH + 2,)),
+            dma((2, KVH, SLOTS_SEEN)),
+            dma((2, KVH, SLOTS_SEEN)),
             dma((KVH, SLOTS_SEEN)),
             dma((KVH, SLOTS_SEEN)),
             dma((KVH,)),
             dma((KVH,)),
         ],
         compiler_params=pltpu.CompilerParams(
-            collective_id=0, has_side_effects=True, vmem_limit_bytes=40 * 1024 * 1024
+            collective_id=0, has_side_effects=True, vmem_limit_bytes=VMEM_BYTES
         ),
     )(order, *[a[0] for a in arrays])
+    outs = pl.pallas_call(
+        settle,
+        out_shape=[jax.ShapeDtypeStruct(out.shape, out.dtype) for out in outs],
+        in_specs=[in_hbm] * 4,
+        out_specs=[in_hbm] * 4,
+        scratch_shapes=[pltpu.VMEM(out.shape, out.dtype) for out in outs] + [dma((2, 4))],
+        compiler_params=pltpu.CompilerParams(vmem_limit_bytes=VMEM_BYTES),
+    )(*outs)
     return tuple(out[None] for out in outs)
 
 

time: 64.4 us -> 49.8 us (0.77)
  the two profiles are of different devices: /device:TPU:29 before, /device:TPU:2 now
where the time goes in v2:
time: 49.8 us; the launch traced here: 49.6 us
  Pallas kernels  49 us (98%)
  between operations  0.64 us (1%)
    pallas_call x1, Pallas kernels, local(): pl.pallas_call(kernel, out_shape=[jax.ShapeDtypeStruct(s, bf16) for s in...  46.9 us
    pallas_call x1, Pallas kernels, local(): pl.pallas_call(settle, out_shape=[jax.ShapeDtypeStruct(out.shape, out.dty...  2.11 us

profile of v2, /device:TPU:2, one launch (start us, length us, event | category | flops | bytes accessed | tf_op | source)
XLA Modules:
  0.0 49.6 jit_solution(14224917303129194225)
XLA Ops:
  0.6 46.9 %shard_map.111 = (bf16[64,4096]{1,0:T(8,128)(2,1)}, bf16[64,4096]{1,0:T(8,128)(2,1)}, bf16[64,512]{1,0:T(8,128)(2,1)}, bf16[64,512]{1,0:T(8,128)(2,1)}) custom-call(s32[64]{0:T(128)} %order.1, bf16[64,4096]{1,0:T(8,128)(2,1)} %bitcast.11, bf16[64,512]{1,0:T(8,128)(2,1)} %bitcast.14, bf16[64,512]{1,0:T(8,128)(2,1)} %bitcast.15, bf16[64,4096]{1,0:T(8,128)(2,1)} %bitcast.12, ...), custom_call_target="tpu_custom_call" | custom-call | tf_op jit(solution)/shard_map/pallas_call | solution.py:387
  47.5 2.1 %shard_map.112 = (bf16[64,4096]{1,0:T(8,128)(2,1)}, bf16[64,4096]{1,0:T(8,128)(2,1)}, bf16[64,512]{1,0:T(8,128)(2,1)}, bf16[64,512]{1,0:T(8,128)(2,1)}) custom-call(bf16[64,4096]{1,0:T(8,128)(2,1)} %get-tuple-element.12.refs_0_, bf16[64,4096]{1,0:T(8,128)(2,1)} %get-tuple-element.13.refs_1_, bf16[64,512]{1,0:T(8,128)(2,1)} %get-tuple-element.14.refs_2_, ...), custom_call_target="tpu_custom_call" | custom-call | tf_op jit(solution)/shard_map/pallas_call | solution.py:419

commit v3 on v2

--- a/solution.py
+++ b/solution.py
@@ -20,35 +20,65 @@
 SCALE = HEAD ** -0.5
 SCALE2 = SCALE * math.log2(math.e)
 VMEM_BYTES = 60 * 1024 * 1024
-UNITS = ((0, 0, 1), (0, 1, 1), (0, 2, 1), (0, 3, 1), (1, 0, 2), (1, 2, 2))
-PAIRED = ((0, 0, 1), (0, 2, 1), )
-RETURNS = ("r1", "t7", "t6", "t45", "t5", "t3", "t4")
+TREES = (
+    (
+        {1: (0, 0, "P"), 2: (0, 0, "U"), 3: (1, 2, "X"), 4: (0, 2, "P"), 5: (1, 2, "D"), 6: (0, 3, "U"), 7: (0, 5, "U")},
+        {1: (1, 0, "P"), 2: (1, 0, "U"), 3: (0, 0, "X"), 4: (1, 3, "P"), 5: (0, 2, "X"), 6: (1, 1, "U"), 7: (0, 1, "ZX")},
+    ),
+    (
+        {1: (0, 0, "P"), 2: (0, 0, "U"), 3: (1, 2, "X"), 4: (0, 2, "P"), 5: (1, 1, "ZX"), 6: (0, 3, "U"), 7: (0, 5, "U")},
+        {1: (1, 0, "P"), 2: (1, 0, "U"), 3: (0, 0, "X"), 4: (1, 3, "P"), 5: (1, 3, "U"), 6: (1, 1, "U"), 7: (1, 4, "U")},
+    ),
+    (
+        {1: (0, 0, "P"), 2: (0, 0, "U"), 3: (1, 0, "ZX"), 4: (0, 2, "P"), 5: (1, 2, "D"), 6: (1, 2, "ZX"), 7: (0, 3, "ZP")},
+        {1: (1, 0, "P"), 2: (1, 0, "U"), 3: (0, 0, "X"), 4: (1, 3, "P"), 5: (0, 2, "X"), 6: (1, 1, "U"), 7: (0, 1, "ZX")},
+    ),
+)
+UNITS = ((0, 0, 1, 0), (0, 1, 1, 0), (0, 2, 1, 0), (0, 3, 1, 0), (1, 0, 2, 1), (1, 2, 2, 1))
+BACK = (2, 2, 2, 2)
+WAYS = tuple(sorted({way for tree in TREES for slots in tree for _, _, way in slots.values()}))
+
+
+def fed(tree, parity, slot):
+    found = [
+        (p, r, way) for p in range(2) for r, (q, source, way) in tree[p].items() if (q, source) == (parity, slot)
+    ]
+    return sorted(found, key=lambda f: -chain(tree, f[0], f[1]))
+
+
+def chain(tree, parity, slot):
+    return 1 + max([chain(tree, p, r) for p, r, _ in fed(tree, parity, slot)], default=0)
+
+
 EVEN = (
-    (("own", 3), ("own", 2), ("own", 0), ("own", 1), ("own", 5), ("f2", 2), ("f2", 0), ("f3", 0), ("own", 4),
-     ("f3", 2), ("f2", 1), ("f7", 0), ("f3", 1), ("f2", 3), ("f7", 1), ("f7", 2), ("f2", 5), ("f3", 3), ("f2", 4),
-     ("last", 0),),
-    (("f7", 3), ("r1", 0), ("last", 1),),
-    (("r1", 1), ("last", 2), ("f3", 4),),
-    (("t7", 0), ("t6", 0), ("f7", 4), ("r1", 2), ("last", 3),),
-    (("r1", 3), ("t7", 1), ("f3", 5), ("t7", 2), ("t6", 1), ("t45", 1), ("f7", 5), ("last", 4),),
-    (("t7", 3), ("t6", 2),),
-    (("last", 5), ("t45", 0), ("t6", 3),),
-    (("t45", 3), ("t45", 2),),
+    (("fwd", 0, 3), ("fwd", 0, 0), ("fwd", 0, 1), ("fwd", 0, 4), ("fwd", 0, 2), ("fwd", 2, 0), ("fwd", 1, 0),
+     ("fwd", 0, 5), ("fwd", 1, 1), ("fwd", 2, 4), ("fwd", 3, 0), ("fwd", 2, 2), ("fwd", 5, 0), ("fwd", 2, 1),
+     ("fwd", 1, 2), ("fwd", 2, 3), ("fwd", 3, 1), ("fwd", 1, 3), ("fwd", 5, 1), ("fwd", 3, 2), ("fwd", 2, 5),
+     ("last", 0, 0),),
+    (("fwd", 5, 2), ("fwd", 5, 4), ("ret", 4, 0), ("ret", 7, 0), ("ret", 5, 0), ("ret", 6, 0), ("last", 0, 1),
+     ("fwd", 3, 3), ("fwd", 5, 3),),
+    (("fwd", 3, 4), ("ret", 7, 1), ("ret", 6, 1), ("ret", 5, 1), ("ret", 4, 1), ("last", 0, 2),),
+    (("fwd", 5, 5), ("ret", 3, 0), ("ret", 7, 2), ("fwd", 3, 5), ("ret", 5, 2), ("ret", 6, 2), ("last", 0, 3),),
+    (("ret", 7, 3), ("ret", 5, 3), ("ret", 4, 3), ("ret", 6, 3), ("ret", 3, 1), ("last", 0, 4), ("ret", 4, 2),),
     (),
+    (("ret", 2, 0), ("ret", 2, 1), ("ret", 1, 0), ("ret", 1, 1), ("last", 0, 5), ("ret", 3, 2),),
+    (("ret", 1, 3), ("ret", 1, 2), ("ret", 3, 3),),
+    (("ret", 2, 2), ("ret", 2, 3),),
 )
 ODD = (
-    (("own", 0), ("own", 1), ("own", 2), ("own", 3), ("own", 4), ("f2", 0), ("f1", 1), ("f2", 1), ("f1", 0),
-     ("f3", 0), ("f2", 2), ("f1", 3), ("own", 5), ("f1", 2), ("f2", 3), ("f3", 1), ("f6", 1), ("f7", 0), ("f6", 0),
-     ("f1", 4), ("f3", 3), ("f6", 3), ("f7", 1), ("f1", 5), ("f3", 2), ("f2", 4), ("last", 0), ("f3", 4), ("f7", 2),
-     ("f6", 2),),
-    (("f6", 4), ("f7", 3), ("f2", 5), ("last", 1),),
-    (("f3", 5), ("r1", 1), ("f6", 5), ("f7", 4), ("last", 2), ("r1", 0),),
-    (("r1", 2), ("last", 3),),
-    (("t7", 0), ("r1", 3), ("t7", 2), ("t3", 0), ("last", 4), ("t5", 0), ("f7", 5),),
-    (("t4", 0), ("t5", 1), ("t7", 1), ("t7", 3), ("t5", 2),),
-    (("t4", 2), ("t6", 0), ("last", 5), ("t5", 3), ("t3", 1),),
-    (("t3", 2), ("t6", 2), ("t4", 1), ("t6", 1),),
-    (("t4", 3), ("t3", 3), ("t6", 3),),
+    (("fwd", 0, 0), ("fwd", 0, 1), ("fwd", 0, 2), ("fwd", 0, 4), ("fwd", 2, 0), ("fwd", 1, 0), ("fwd", 0, 3),
+     ("fwd", 2, 1), ("fwd", 2, 2), ("fwd", 1, 1), ("fwd", 1, 2), ("fwd", 3, 0), ("fwd", 0, 5), ("fwd", 1, 4),
+     ("fwd", 1, 3), ("fwd", 3, 1), ("fwd", 2, 3), ("fwd", 3, 2), ("fwd", 2, 4), ("last", 0, 0), ("fwd", 1, 5),
+     ("fwd", 3, 4),),
+    (("fwd", 2, 5), ("fwd", 3, 3), ("fwd", 3, 5), ("last", 0, 1),),
+    (("ret", 5, 1), ("last", 0, 2), ("ret", 7, 0),),
+    (("ret", 6, 1), ("ret", 7, 1), ("fwd", 4, 4), ("last", 0, 3), ("ret", 5, 0), ("ret", 4, 0), ("ret", 6, 0),),
+    (("ret", 7, 3), ("ret", 6, 2), ("ret", 4, 3), ("ret", 4, 2), ("fwd", 4, 5), ("ret", 5, 2), ("ret", 5, 3),
+     ("ret", 7, 2), ("ret", 4, 1), ("ret", 3, 0), ("last", 0, 4),),
+    (("ret", 2, 0), ("ret", 3, 3),),
+    (("ret", 6, 3), ("ret", 1, 2), ("last", 0, 5),),
+    (("ret", 3, 1), ("ret", 1, 1), ("ret", 2, 1), ("ret", 3, 2),),
+    (("ret", 1, 0), ("ret", 2, 3), ("ret", 1, 3), ("ret", 2, 2),),
 )
 MESH = pl.DeviceIdType.MESH
 
@@ -72,18 +102,35 @@
     uly = lax.axis_index("uly")
     y_hi = lax.rem(blk, 2)
     z, planes = blk // 2, blks // 2
-    even = y_hi == 0
-    odd = y_hi == 1
 
     partner = {"uly": 1 - uly}
-    cross = {"blk": blk + 1 - 2 * y_hi, "uly": 1 - uly}
-    above = {"blk": lax.rem(blk + 2, blks)}
-    below = {"blk": lax.rem(blk + blks - 2, blks)}
+    flip = blk + 1 - 2 * y_hi
+
+    def ring(group):
+        return lax.rem(group + 2 * blks, blks)
+
+    up = {
+        "P": partner,
+        "X": {"blk": flip, "uly": 1 - uly},
+        "D": {"blk": flip},
+        "U": {"blk": ring(blk + 2)},
+        "ZP": {"blk": ring(blk + 2), "uly": 1 - uly},
+        "ZX": {"blk": ring(flip + 2), "uly": 1 - uly},
+        "ZZX": {"blk": ring(flip + 4), "uly": 1 - uly},
+    }
+    down = dict(
+        up,
+        U={"blk": ring(blk - 2)},
+        ZP={"blk": ring(blk - 2), "uly": 1 - uly},
+        ZX={"blk": ring(flip - 2), "uly": 1 - uly},
+        ZZX={"blk": ring(flip - 4), "uly": 1 - uly},
+    )
     after = {"pipe": lax.rem(pipe + 1, pipes)}
     before = {"pipe": lax.rem(pipe + pipes - 1, pipes)}
 
     barrier = pltpu.get_barrier_semaphore()
-    for peer in (partner, cross, above, below, after, before):
+    peers = [up[way] for way in WAYS] + [down[way] for way in WAYS if way not in "PXD"] + [after, before]
+    for peer in peers:
         pl.semaphore_signal(barrier, inc=1, device_id=peer, device_id_type=MESH)
 
     kv_loads = {}
@@ -106,99 +153,68 @@
     for load in loads:
         load.start()
 
-    target = {1: partner, 2: above, 3: cross, 4: partner, 5: cross, 6: above, 7: above}
-    back = {1: partner, 2: below, 3: cross, 4: partner, 5: cross, 6: below, 7: below}
-
-    def paired(unit):
-        return unit in PAIRED
-
-    def message(unit, r, source):
-        phase, head, count = unit
+    def message(unit, parity, r, way, source=0):
+        phase, head, count, _ = unit
         kv = (kvb, kvf)[phase]
         return pltpu.make_async_remote_copy(
             src_ref=kv.at[source, pl.ds(head, count)],
             dst_ref=kv.at[r, pl.ds(head, count)],
-            send_sem=g_send.at[phase, head, r],
+            send_sem=g_send.at[phase, head, parity, r],
             recv_sem=g_recv.at[phase, head, r],
-            device_id=partner if r == 7 and paired(unit) else target[r],
+            device_id=up[way],
             device_id_type=MESH,
         )
 
-    def forward(unit, arrived, *sends):
-        if arrived:
-            message(unit, arrived, 0).wait_recv()
-        for r in sends:
-            message(unit, r, arrived).start()
-
-    def own_slot(unit, *sends):
-        phase, head, count = unit
-        for g in range(head, head + count):
-            for load in kv_loads[phase, g]:
-                load.wait()
-        forward(unit, 0, *sends)
-
-    def last_slots(unit, *slots):
-        for r in slots:
-            forward(unit, r)
-
-    def term(g, r):
+    def arrived(unit, r):
+        message(unit, 0, r, "P").wait_recv()
+
+    def send_on(unit, parity, slot):
+        phase, head, count, tree = unit
+        if slot:
+            arrived(unit, slot)
+        else:
+            for g in range(head, head + count):
+                for load in kv_loads[phase, g]:
+                    load.wait()
+        for p, r, way in fed(TREES[tree], parity, slot):
+            message(unit, p, r, way, slot).start()
+
+    def wait_others(unit, parity, _):
+        for r in range(1, SLOTS_SEEN):
+            if not fed(TREES[unit[3]], parity, r):
+                arrived(unit, r)
+
+    def term(g, parity, r):
         return pltpu.make_async_remote_copy(
             src_ref=part.at[g, r],
-            dst_ref=got.at[g, r],
+            dst_ref=got.at[g, parity, r],
             send_sem=r_send.at[g, r],
-            recv_sem=r_recv.at[g, r],
-            device_id=back[r],
+            recv_sem=r_recv.at[g, parity, r],
+            device_id=down[TREES[BACK[g]][parity][r][2]],
             device_id_type=MESH,
         )
 
-    def take(g, r, into):
-        term(g, r).wait_recv()
-        part[g, into] = (
-            part[g, into].astype(jnp.float32) + got[g, r].astype(jnp.float32)
-        ).astype(jnp.bfloat16)
-
-    def gather_moves(unit):
-        pair = paired(unit)
-        return {
-            "own": (lambda: own_slot(unit, 3, 2, 1), lambda: own_slot(unit, 2, 1)),
-            "f1": (None, lambda: forward(unit, 1, 6)),
-            "f2": (lambda: forward(unit, 2, 5, 4), lambda: forward(unit, 2, 3)),
-            "f3": (lambda: forward(unit, 3, 6), lambda: forward(unit, 3, 4)),
-            "f6": (None, lambda: forward(unit, 6, 5)),
-            "f7": (lambda: forward(unit, 6 if pair else 5, 7), lambda: forward(unit, 5 if pair else 4, 7)),
-            "last": (
-                lambda: last_slots(unit, 1, 4, 5 if pair else 6, 7),
-                lambda: last_slots(unit, 4 if pair else 5, 7),
-            ),
-        }
-
-    def back_send(g, *slots):
-        for r in slots:
-            term(g, r).start()
-
-    def back_sum(g, into, *slots):
-        for r in slots:
-            take(g, r, into)
-        term(g, into).start()
-
-    def return_moves(g):
-        return {
-            "r1": (lambda: back_send(g, 7, 4, 6, 1), lambda: back_send(g, 5, 7)),
-            "t7": (lambda: back_sum(g, 5, 7), lambda: back_sum(g, 4, 7)),
-            "t6": (lambda: back_sum(g, 3, 6), lambda: back_sum(g, 1, 6)),
-            "t45": (lambda: back_sum(g, 2, 4, 5), None),
-            "t5": (None, lambda: back_sum(g, 6, 5)),
-            "t3": (None, lambda: back_sum(g, 2, 3)),
-            "t4": (None, lambda: back_sum(g, 3, 4)),
-        }
+    def received(g, parity, slot, sums):
+        for p, r, _ in reversed(fed(TREES[BACK[g]], parity, slot)):
+            term(g, p, r).wait_recv()
+            sums = sums + got[g, p, r].astype(jnp.float32)
+        return sums
+
+    def send_back(g, parity, slot):
+        if fed(TREES[BACK[g]], parity, slot):
+            sums = received(g, parity, slot, part[g, slot].astype(jnp.float32))
+            part[g, slot] = sums.astype(jnp.bfloat16)
+        term(g, parity, slot).start()
 
     def run(k):
         for parity, table in enumerate((EVEN, ODD)):
             @pl.when(y_hi == parity)
             def _():
-                for name, index in table[k]:
-                    moves = return_moves(index) if name in RETURNS else gather_moves(UNITS[index])
-                    moves[name][parity]()
+                for name, slot, index in table[k]:
+                    if name == "ret":
+                        send_back(index, parity, slot)
+                    else:
+                        {"fwd": send_on, "last": wait_others}[name](UNITS[index], parity, slot)
 
     y = 2 * y_hi + uly
     col_p, col_x, col_d = 2 * y_hi + 1 - uly, 3 - y, 2 * (1 - y_hi) + uly
@@ -287,7 +303,7 @@
         def _():
             hand(g).start()
 
-    pl.semaphore_wait(barrier, 6)
+    pl.semaphore_wait(barrier, len(peers))
     run(0)
     for load in loads:
         load.wait()
@@ -316,21 +332,12 @@
 
     lax.fori_loop(0, 2 * KVH, step, 0)
 
-    for g in range(KVH):
-        sums = own[g]
-        for r in (1, 2):
-            term(g, r).wait_recv()
-            sums = sums + got[g, r].astype(jnp.float32)
-
-        @pl.when(odd)
+    for parity in range(2):
+        @pl.when(y_hi == parity)
         def _():
-            total[:, :, g * HEAD:(g + 1) * HEAD] = sums.astype(jnp.bfloat16)
-
-        @pl.when(even)
-        def _():
-            term(g, 3).wait_recv()
-            full = sums + got[g, 3].astype(jnp.float32)
-            total[:, :, g * HEAD:(g + 1) * HEAD] = full.astype(jnp.bfloat16)
+            for g in range(KVH):
+                sums = received(g, parity, 0, own[g])
+                total[:, :, g * HEAD:(g + 1) * HEAD] = sums.astype(jnp.bfloat16)
 
     stores = [
         pltpu.make_async_copy(total.at[0], dk_out, out_sem.at[2 * KVH]),
@@ -341,10 +348,14 @@
     for g in range(KVH):
         grad_copy(g).wait()
         for r in range(1, SLOTS_SEEN):
-            term(g, r).wait_send()
-    for unit in UNITS:
-        for r in range(1, SLOTS_SEEN):
-            message(unit, r, 0).wait_send()
+            term(g, 0, r).wait_send()
+    for parity in range(2):
+        @pl.when(y_hi == parity)
+        def _():
+            for unit in UNITS:
+                for slot in range(SLOTS_SEEN):
+                    for p, r, way in fed(TREES[unit[3]], parity, slot):
+                        message(unit, p, r, way).wait_send()
 
     @pl.when(pipe < pipes - 1)
     def _():
@@ -399,16 +410,16 @@
             pltpu.VMEM(wide, bf16),
             pltpu.VMEM((KVH, SLOTS_SEEN, 2, TOK, HEAD), bf16),
             pltpu.VMEM((KVH, 2, TOK, HEAD), jnp.float32),
-            pltpu.VMEM((KVH, SLOTS_SEEN, 2, TOK, HEAD), bf16),
+            pltpu.VMEM((KVH, 2, SLOTS_SEEN, 2, TOK, HEAD), bf16),
             pltpu.VMEM((2,) + narrow, bf16),
             pltpu.VMEM((TOK, WIDE), bf16),
             dma((3,)),
             dma((2, KVH, 2)),
             dma((2 * KVH + 2,)),
-            dma((2, KVH, SLOTS_SEEN)),
+            dma((2, KVH, 2, SLOTS_SEEN)),
             dma((2, KVH, SLOTS_SEEN)),
             dma((KVH, SLOTS_SEEN)),
-            dma((KVH, SLOTS_SEEN)),
+            dma((KVH, 2, SLOTS_SEEN)),
             dma((KVH,)),
             dma((KVH,)),
         ],

time: 49.8 us -> 47.1 us (0.946)
  the two profiles are of different devices: /device:TPU:2 before, /device:TPU:4 now
where the time goes in v3:
time: 47.1 us; the launch traced here: 46.9 us
  Pallas kernels  46.3 us (98%)
  between operations  0.64 us (1%)
    pallas_call x1, Pallas kernels, local(): pl.pallas_call(kernel, out_shape=[jax.ShapeDtypeStruct(s, bf16) for s in...  44.2 us
    pallas_call x1, Pallas kernels, local(): pl.pallas_call(settle, out_shape=[jax.ShapeDtypeStruct(out.shape, out.dty...  2.11 us

profile of v3, /device:TPU:4, one launch (start us, length us, event | category | flops | bytes accessed | tf_op | source)
XLA Modules:
  0.0 46.9 jit_solution(5627442267665289782)
XLA Ops:
  0.6 44.2 %shard_map.111 = (bf16[64,4096]{1,0:T(8,128)(2,1)}, bf16[64,4096]{1,0:T(8,128)(2,1)}, bf16[64,512]{1,0:T(8,128)(2,1)}, bf16[64,512]{1,0:T(8,128)(2,1)}) custom-call(s32[64]{0:T(128)} %order.1, bf16[64,4096]{1,0:T(8,128)(2,1)} %bitcast.11, bf16[64,512]{1,0:T(8,128)(2,1)} %bitcast.14, bf16[64,512]{1,0:T(8,128)(2,1)} %bitcast.15, bf16[64,4096]{1,0:T(8,128)(2,1)} %bitcast.12, ...), custom_call_target="tpu_custom_call" | custom-call | tf_op jit(solution)/shard_map/pallas_call | solution.py:398
  44.8 2.1 %shard_map.112 = (bf16[64,4096]{1,0:T(8,128)(2,1)}, bf16[64,4096]{1,0:T(8,128)(2,1)}, bf16[64,512]{1,0:T(8,128)(2,1)}, bf16[64,512]{1,0:T(8,128)(2,1)}) custom-call(bf16[64,4096]{1,0:T(8,128)(2,1)} %get-tuple-element.12.refs_0_, bf16[64,4096]{1,0:T(8,128)(2,1)} %get-tuple-element.13.refs_1_, bf16[64,512]{1,0:T(8,128)(2,1)} %get-tuple-element.14.refs_2_, ...), custom_call_target="tpu_custom_call" | custom-call | tf_op jit(solution)/shard_map/pallas_call | solution.py:430

commit v4 on v3

--- a/solution.py
+++ b/solution.py
@@ -1,3 +1,4 @@
+import functools
 import functools
 import math
 
@@ -53,7 +54,7 @@
 EVEN = (
     (("fwd", 0, 3), ("fwd", 0, 0), ("fwd", 0, 1), ("fwd", 0, 4), ("fwd", 0, 2), ("fwd", 2, 0), ("fwd", 1, 0),
      ("fwd", 0, 5), ("fwd", 1, 1), ("fwd", 2, 4), ("fwd", 3, 0), ("fwd", 2, 2), ("fwd", 5, 0), ("fwd", 2, 1),
-     ("fwd", 1, 2), ("fwd", 2, 3), ("fwd", 3, 1), ("fwd", 1, 3), ("fwd", 5, 1), ("fwd", 3, 2), ("fwd", 2, 5),
+     ("fwd", 1, 2), ("fwd", 2, 3), ("fwd", 3, 1), ("fwd", 5, 1), ("fwd", 3, 2), ("fwd", 2, 5), ("fwd", 1, 3),
      ("last", 0, 0),),
     (("fwd", 5, 2), ("fwd", 5, 4), ("ret", 4, 0), ("ret", 7, 0), ("ret", 5, 0), ("ret", 6, 0), ("last", 0, 1),
      ("fwd", 3, 3), ("fwd", 5, 3),),
@@ -72,9 +73,10 @@
      ("fwd", 3, 4),),
     (("fwd", 2, 5), ("fwd", 3, 3), ("fwd", 3, 5), ("last", 0, 1),),
     (("ret", 5, 1), ("last", 0, 2), ("ret", 7, 0),),
-    (("ret", 6, 1), ("ret", 7, 1), ("fwd", 4, 4), ("last", 0, 3), ("ret", 5, 0), ("ret", 4, 0), ("ret", 6, 0),),
-    (("ret", 7, 3), ("ret", 6, 2), ("ret", 4, 3), ("ret", 4, 2), ("fwd", 4, 5), ("ret", 5, 2), ("ret", 5, 3),
-     ("ret", 7, 2), ("ret", 4, 1), ("ret", 3, 0), ("last", 0, 4),),
+    (("ret", 6, 1), ("ret", 7, 1), ("fwd", 4, 4), ("last", 0, 3), ("ret", 5, 0), ("ret", 5, 2), ("ret", 4, 0),
+     ("ret", 6, 0),),
+    (("ret", 7, 3), ("ret", 6, 2), ("ret", 4, 3), ("ret", 4, 2), ("fwd", 4, 5), ("ret", 5, 3), ("ret", 7, 2),
+     ("ret", 4, 1), ("ret", 3, 0), ("last", 0, 4),),
     (("ret", 2, 0), ("ret", 3, 3),),
     (("ret", 6, 3), ("ret", 1, 2), ("last", 0, 5),),
     (("ret", 3, 1), ("ret", 1, 1), ("ret", 2, 1), ("ret", 3, 2),),
@@ -231,7 +233,7 @@
         o * plane[2] + y_hi * plane[1] + col_d,
     ]
     mine = order[held[0]]
-    offsets = [None] + [jnp.where(order[held[r]] < mine, 0.0, NEG) for r in range(1, SLOTS_SEEN)]
+    offsets = [0.0] + [jnp.where(order[held[r]] < mine, 0.0, NEG) for r in range(1, SLOTS_SEEN)]
 
     def stacked(ref, g):
         return jnp.concatenate(
@@ -242,14 +244,16 @@
         return ref[:, g, c].reshape(KEYS, HEAD)
 
     def raised(k, q):
-        raw = dot(k, q, NT) * SCALE2
-        key = lax.broadcasted_iota(jnp.int32, (TOK, ROWS), 0)
-        row = lax.broadcasted_iota(jnp.int32, (TOK, ROWS), 1) % TOK
-        pieces = [jnp.where(key <= row, raw[:TOK], NEG)]
-        for r in range(1, SLOTS_SEEN):
-            pieces.append(raw[r * TOK:(r + 1) * TOK] + offsets[r])
-        scores = jnp.concatenate(pieces, axis=0)
-        p = jnp.exp2(scores - jnp.max(scores, axis=0, keepdims=True))
+        raw = dot(k, q, NT)
+        key = lax.broadcasted_iota(jnp.int32, (TOK, q.shape[0]), 0)
+        row = lax.broadcasted_iota(jnp.int32, (TOK, q.shape[0]), 1) % TOK
+        blocks = [jnp.where(key <= row, raw[:TOK], NEG)]
+        blocks += [raw[r * TOK:(r + 1) * TOK] for r in range(1, SLOTS_SEEN)]
+        peaks = [jnp.max(block, axis=0, keepdims=True) + offset for block, offset in zip(blocks, offsets)]
+        peak = functools.reduce(jnp.maximum, peaks)
+        p = jnp.concatenate(
+            [jnp.exp2((block - (peak - offset)) * SCALE2) for block, offset in zip(blocks, offsets)], axis=0
+        )
         return p, 1.0 / jnp.sum(p, axis=0, keepdims=True)
 
     def spread(ref, g, value):
@@ -378,15 +382,22 @@
 
 def settle(*refs):
     ins, outs, held, sems = refs[:4], refs[4:8], refs[8:12], refs[12]
-    fetched = [pltpu.make_async_copy(ins[i], held[i], sems.at[0, i]) for i in range(4)]
-    stored = [pltpu.make_async_copy(held[i], outs[i], sems.at[1, i]) for i in range(4)]
-    for copy in fetched:
-        copy.start()
-    for fetch, store in zip(fetched, stored):
+    moves = []
+    for i, pieces in enumerate((4, 4, 1, 1)):
+        rows = TOK // pieces
+        for piece in range(pieces):
+            here, slot = pl.ds(piece * rows, rows), len(moves)
+            moves.append((
+                pltpu.make_async_copy(ins[i].at[here], held[i].at[here], sems.at[0, slot]),
+                pltpu.make_async_copy(held[i].at[here], outs[i].at[here], sems.at[1, slot]),
+            ))
+    for fetch, _ in moves:
+        fetch.start()
+    for fetch, store in moves:
         fetch.wait()
         store.start()
-    for copy in stored:
-        copy.wait()
+    for _, store in moves:
+        store.wait()
 
 
 def local(order, *arrays):
@@ -432,7 +443,7 @@
         out_shape=[jax.ShapeDtypeStruct(out.shape, out.dtype) for out in outs],
         in_specs=[in_hbm] * 4,
         out_specs=[in_hbm] * 4,
-        scratch_shapes=[pltpu.VMEM(out.shape, out.dtype) for out in outs] + [dma((2, 4))],
+        scratch_shapes=[pltpu.VMEM(out.shape, out.dtype) for out in outs] + [dma((2, 10))],
         compiler_params=pltpu.CompilerParams(vmem_limit_bytes=VMEM_BYTES),
     )(*outs)
     return tuple(out[None] for out in outs)

time: 47.1 us -> 46.8 us (level)
  the two profiles are of different devices: /device:TPU:4 before, /device:TPU:16 now
where the time goes in v4:
time: 46.8 us; the launch traced here: 46.6 us
  Pallas kernels  46 us (98%)
  between operations  0.64 us (1%)
    pallas_call x1, Pallas kernels, local(): pl.pallas_call(kernel, out_shape=[jax.ShapeDtypeStruct(s, bf16) for s in...  43.8 us
    pallas_call x1, Pallas kernels, local(): pl.pallas_call(settle, out_shape=[jax.ShapeDtypeStruct(out.shape, out.dty...  2.16 us

profile of v4, /device:TPU:16, one launch (start us, length us, event | category | flops | bytes accessed | tf_op | source)
XLA Modules:
  0.0 46.6 jit_solution(3414270435255044607)
XLA Ops:
  0.6 43.8 %shard_map.111 = (bf16[64,4096]{1,0:T(8,128)(2,1)}, bf16[64,4096]{1,0:T(8,128)(2,1)}, bf16[64,512]{1,0:T(8,128)(2,1)}, bf16[64,512]{1,0:T(8,128)(2,1)}) custom-call(s32[64]{0:T(128)} %order.1, bf16[64,4096]{1,0:T(8,128)(2,1)} %bitcast.11, bf16[64,512]{1,0:T(8,128)(2,1)} %bitcast.14, bf16[64,512]{1,0:T(8,128)(2,1)} %bitcast.15, bf16[64,4096]{1,0:T(8,128)(2,1)} %bitcast.12, ...), custom_call_target="tpu_custom_call" | custom-call | tf_op jit(solution)/shard_map/pallas_call | solution.py:409
  44.4 2.2 %shard_map.112 = (bf16[64,4096]{1,0:T(8,128)(2,1)}, bf16[64,4096]{1,0:T(8,128)(2,1)}, bf16[64,512]{1,0:T(8,128)(2,1)}, bf16[64,512]{1,0:T(8,128)(2,1)}) custom-call(bf16[64,4096]{1,0:T(8,128)(2,1)} %get-tuple-element.12.refs_0_, bf16[64,4096]{1,0:T(8,128)(2,1)} %get-tuple-element.13.refs_1_, bf16[64,512]{1,0:T(8,128)(2,1)} %get-tuple-element.14.refs_2_, ...), custom_call_target="tpu_custom_call" | custom-call | tf_op jit(solution)/shard_map/pallas_call | solution.py:441
